TPU v7x, 128 devices: a whole 4x4x4 slice. The times are simulated.
128 devices in a mesh: llm: 16 (over y, x), enc: 8 (over z, core).
Axes of the slice: x: 4, y: 4, z: 4, core: 2. Of those that a mesh axis runs over, the one named last changes fastest.
Arguments:
- patches: bfloat16 [16384, 1152], P(('llm', 'enc')), may hold values from -6 to 6
- image_seg: int32 [128, 1, 128], replicated, may hold values from 0 to 3, never falling along the last dimension, each value on 1 to 64 neighbouring positions
- owner_slot: int32 [128, 1], replicated, may hold values from 0 to 15, as said below
- place_start: int32 [128, 1], P(('llm', 'enc')), may hold values from 0 to 32, as said below
- text_embeds: bfloat16 [20480, 1280], P(('llm', 'enc')), may hold values from -6 to 6
- merged_grad: bfloat16 [20480, 1280], P(('llm', 'enc')), may hold values from -0.4375 to 0.4375
- w_patch: bfloat16 [1152, 1280], replicated, may hold values from -0.1875 to 0.1875
- w_qkv: bfloat16 [1280, 3840], replicated, may hold values from -1.118034 to 1.118034
- w_out: bfloat16 [1280, 1280], replicated, may hold values from -0.15625 to 0.15625
Outputs:
- merged: bfloat16 [20480, 1280], P(('llm', 'enc'))
- grad_patch: float32 [1152, 1280], P(None, ('llm', 'enc'))
- grad_out: float32 [1280, 1280], P(None, ('llm', 'enc'))
Inputs may be any that keep to these rules, and one draw needn't show every extreme that they name: `image_seg`: within each sample's block of 128 rows, image numbers start at 0 and never fall. `owner_slot`: a value q + m names LLM rank q (device on the same enc index) and its placeholder block m; the samples of one device name distinct ranks; among the devices of one enc index every pair of rank and block is named exactly once. `place_start`: block m starts between m * 160 and m * 160 + 32.
All inputs are finite; a program needn't handle non-finite values.
Results may differ from a plain program's by a relative error of at most 0.014.
Values may be sent and summed in bfloat16 or wider, within the bound.
A program may use at most 128 MiB of HBM per device.

v0:
```python
import jax
import jax.numpy as jnp
from jax import lax
from jax.sharding import PartitionSpec as P

D = 1280
HEADS = 16
HEAD_DIM = 80


CONTRACT_ROWS = (((0,), (0,)), ((), ()))
CONTRACT_COLS = (((1,), (1,)), ((), ()))


def layer_norm(values_in):
    average = jnp.mean(values_in, axis=-1, keepdims=True)
    centred = values_in - average
    inverse_std = lax.rsqrt(jnp.mean(centred * centred, axis=-1, keepdims=True) + 1e-06)
    return (centred * inverse_std, inverse_std)


def split_heads(packed, blocks, length):
    return packed.reshape(blocks, length, HEADS, HEAD_DIM)


def attention_forward(qkv_low, segments):
    blocks, length = segments.shape
    queries = split_heads(qkv_low[:, :, :D], blocks, length)
    keys_all = split_heads(qkv_low[:, :, D : 2 * D], blocks, length)
    values_all = split_heads(qkv_low[:, :, 2 * D :], blocks, length)
    scores = jnp.einsum(
        "bqhe,bkhe->bhqk", queries, keys_all, preferred_element_type=jnp.float32
    ) * HEAD_DIM ** (-0.5)
    same_image = segments[:, None, :, None] == segments[:, None, None, :]
    scores = jnp.where(same_image, scores, jnp.float32(-1e30))
    row_max = jnp.max(scores, axis=-1, keepdims=True)
    weights = jnp.exp(scores - row_max)
    probability = weights / jnp.sum(weights, axis=-1, keepdims=True)
    probs_low = probability.astype(jnp.bfloat16)
    attended = jnp.einsum(
        "bhqk,bkhe->bqhe", probs_low, values_all, preferred_element_type=jnp.float32
    )
    attn_cache = (queries, keys_all, values_all, probability, probs_low)
    return (attended.reshape(blocks, length, D).astype(jnp.bfloat16), attn_cache)


def attention_backward(attn_cache, grad_attended):
    queries, keys_all, values_all, probability, probs_low = attn_cache
    blocks, length = (grad_attended.shape[0], grad_attended.shape[1])
    grad_heads = split_heads(grad_attended, blocks, length)
    grad_prob = jnp.einsum(
        "bqhe,bkhe->bhqk", grad_heads, values_all, preferred_element_type=jnp.float32
    )
    grad_score = probability * (
        grad_prob - jnp.sum(grad_prob * probability, axis=-1, keepdims=True)
    )
    score_low = (grad_score * HEAD_DIM ** (-0.5)).astype(jnp.bfloat16)
    grad_query = jnp.einsum(
        "bhqk,bkhe->bqhe", score_low, keys_all, preferred_element_type=jnp.float32
    )
    grad_key = jnp.einsum("bhqk,bqhe->bkhe", score_low, queries, preferred_element_type=jnp.float32)
    grad_value = jnp.einsum(
        "bhqk,bqhe->bkhe", probs_low, grad_heads, preferred_element_type=jnp.float32
    )
    joined = jnp.concatenate(
        [
            grad_query.reshape(blocks, length, D),
            grad_key.reshape(blocks, length, D),
            grad_value.reshape(blocks, length, D),
        ],
        axis=-1,
    )
    return joined.astype(jnp.bfloat16)


def encode(patch_block, segments, w_patch, w_qkv, w_out):
    blocks, length = segments.shape
    patch_rows = patch_block.reshape(blocks * length, patch_block.shape[2])
    residual = jnp.dot(patch_rows, w_patch, preferred_element_type=jnp.float32)
    normed, inverse_std = layer_norm(residual)
    normed_low = normed.astype(jnp.bfloat16)
    qkv_low = jnp.dot(normed_low, w_qkv, preferred_element_type=jnp.float32).astype(jnp.bfloat16)
    attended, attn_cache = attention_forward(qkv_low.reshape(blocks, length, 3 * D), segments)
    attended_rows = attended.reshape(blocks * length, D)
    output = residual + jnp.dot(attended_rows, w_out, preferred_element_type=jnp.float32)
    stored = (patch_rows, normed, inverse_std, attended_rows, attn_cache)
    return (output.astype(jnp.bfloat16).reshape(blocks, length, D), stored)


def backprop(stored, upstream, w_qkv, w_out):
    patch_rows, normed, inverse_std, attended_rows, attn_cache = stored
    blocks = attn_cache[3].shape[0]
    length = attn_cache[3].shape[2]
    grad_out = lax.dot_general(
        attended_rows, upstream, CONTRACT_ROWS, preferred_element_type=jnp.float32
    )
    grad_attended = lax.dot_general(
        upstream, w_out, CONTRACT_COLS, preferred_element_type=jnp.float32
    ).astype(jnp.bfloat16)
    grad_qkv_low = attention_backward(attn_cache, grad_attended.reshape(blocks, length, D)).reshape(
        blocks * length, 3 * D
    )
    grad_normed = lax.dot_general(
        grad_qkv_low, w_qkv, CONTRACT_COLS, preferred_element_type=jnp.float32
    )
    mean_grad = jnp.mean(grad_normed, axis=-1, keepdims=True)
    mean_cross = jnp.mean(grad_normed * normed, axis=-1, keepdims=True)
    grad_residual = upstream.astype(jnp.float32) + inverse_std * (
        grad_normed - mean_grad - normed * mean_cross
    )
    grad_patch = lax.dot_general(
        patch_rows,
        grad_residual.astype(jnp.bfloat16),
        CONTRACT_ROWS,
        preferred_element_type=jnp.float32,
    )
    return (grad_patch, grad_out)


def place_blocks(text_rows, blocks_in, starts):

    def write_one(slot_number, current):
        return lax.dynamic_update_slice_in_dim(
            current, blocks_in[slot_number], starts[slot_number], 0
        )

    return lax.fori_loop(0, blocks_in.shape[0], write_one, text_rows)


def take_blocks(grad_rows, starts, length):
    return jax.vmap(lambda offset: lax.dynamic_slice_in_dim(grad_rows, offset, length, 0))(starts)


def shards(
    patches, image_seg, owner_slot, place_start, text_embeds, merged_grad, w_patch, w_qkv, w_out
):
    llm_count = lax.axis_size("llm")
    enc_count = lax.axis_size("enc")
    llm_rank = lax.axis_index("llm")
    column = lax.axis_index("enc")
    groups = place_start.shape[1]
    length = image_seg.shape[2]
    device = llm_rank * enc_count + column
    starts = place_start[0]
    own_slots = lax.dynamic_index_in_dim(owner_slot, device, 0, keepdims=False)
    ranks_list = jnp.arange(llm_count, dtype=jnp.int32)
    send_select = (own_slots[None, :] // groups == ranks_list[:, None]).astype(jnp.bfloat16)
    column_slots = lax.dynamic_index_in_dim(
        owner_slot.reshape(llm_count, enc_count, groups), column, 1, keepdims=False
    )
    slot_list = jnp.arange(groups, dtype=jnp.int32)
    arrival = (column_slots[:, None, :] == llm_rank * groups + slot_list[None, :, None]).astype(
        jnp.int32
    )
    arrive_select = jnp.sum(arrival, axis=2).astype(jnp.bfloat16)
    patch_groups = patches.reshape(groups, length, patches.shape[1])
    own_segments = lax.dynamic_index_in_dim(image_seg, device, 0, keepdims=False)
    embedded, stored = encode(patch_groups, own_segments, w_patch, w_qkv, w_out)
    outgoing = jnp.einsum(
        "qg,grd->qrd", send_select, embedded, preferred_element_type=jnp.float32
    ).astype(jnp.bfloat16)
    returned = lax.all_to_all(outgoing, "llm", split_axis=0, concat_axis=0, tiled=True)
    slot_rows = jnp.einsum(
        "rm,rid->mid", arrive_select, returned, preferred_element_type=jnp.float32
    ).astype(jnp.bfloat16)
    merged = place_blocks(text_embeds, slot_rows, starts)
    slot_grads = take_blocks(merged_grad, starts, length)
    grad_sent = jnp.einsum(
        "rm,mid->rid", arrive_select, slot_grads, preferred_element_type=jnp.float32
    ).astype(jnp.bfloat16)
    grad_back = lax.all_to_all(grad_sent, "llm", split_axis=0, concat_axis=0, tiled=True)
    upstream = jnp.einsum(
        "qg,qrd->grd", send_select, grad_back, preferred_element_type=jnp.float32
    ).astype(jnp.bfloat16)
    grad_patch, grad_out = backprop(stored, upstream.reshape(groups * length, D), w_qkv, w_out)
    totals = (
        lax.psum_scatter(grad_patch, ("llm", "enc"), scatter_dimension=1, tiled=True),
        lax.psum_scatter(grad_out, ("llm", "enc"), scatter_dimension=1, tiled=True),
    )
    return (merged, totals[0], totals[1])


def solution(mesh):
    return jax.shard_map(
        shards,
        mesh=mesh,
        in_specs=(
            P(("llm", "enc"), None),
            P(),
            P(),
            P(("llm", "enc"), None),
            P(("llm", "enc"), None),
            P(("llm", "enc"), None),
            P(),
            P(),
            P(),
        ),
        out_specs=(P(("llm", "enc"), None), P(None, ("llm", "enc")), P(None, ("llm", "enc"))),
        check_vma=False,
    )
```

profile of v0, /device:TPU:1, one launch (start us, length us, event | category | flops | bytes accessed | tf_op | source)
XLA Modules:
  0.0 383.9 jit_solution(14168225632161056199)
XLA Ops:
  7.2 0.0 copy-start
  7.2 1.9 copy.65
  9.1 0.5 broadcast.138
  9.6 1.3 reduce.12
  10.9 0.1 reshape.224
  11.7 0.2 fusion.38
  11.9 1.1 dynamic-slice_convert_fusion
  12.9 3.6 multiply_convert_fusion
  16.5 7.6 %all-to-all-start.1 = ((bf16[16,128,1280]{2,1,0:T(8,128)(2,1)}), bf16[16,128,1280]{2,1,0:T(8,128)(2,1)}, u32[]{:S(2)}, u32[]{:S(2)}) async-start(bf16[16,128,1280]{2,1,0:T(8,128)(2,1)} %multiply_convert_fusion), calls=%async_computation.1 | async-start | bytes 10485760 | tf_op jit(solution)/shard_map/all_to_all | solution.py:171
  24.2 0.0 all-reduce.5.cloned.1.call-start
  24.2 2.6 fusion.56
  26.9 0.0 copy-start.1
  26.9 0.2 multiply_reduce_fusion.2
  27.1 0.0 copy-start.6
  27.1 5.3 %fusion.6 = bf16[1,128,3840]{2,1,0:T(8,128)(2,1)S(1)} fusion(bf16[1280,3840]{1,0:T(8,128)(2,1)} %param.16, f32[128,1280]{1,0:T(8,128)S(1)} %get-tuple-element.37, f32[128]{0:T(128)S(1)} %add_rsqrt_fusion, f32[128]{0:T(128)S(1)} %broadcast_multiply_fusion.2), kind=kOutput, calls=%fused_computation.10 | convolution fusion | flops 1259274240 | bytes 11469824 | tf_op jit(solution)/shard_map/dot_general | solution.py:82
  32.4 0.0 copy-done.1
  32.5 1.0 fusion.55
  33.4 1.9 copy.32
  35.3 1.9 copy.33
  37.2 1.9 copy.34
  39.0 0.0 copy-done.6
  39.0 0.6 constant_dynamic-slice_fusion.1
  39.6 0.7 fusion.42
  40.3 0.6 compare_convert_fusion
  40.9 0.1 broadcast_compare_fusion
  41.0 2.6 fusion.57
  43.6 2.6 convolution_convert_fusion.5
  46.2 55.3 %all-to-all-done.1 = bf16[16,128,1280]{2,1,0:T(8,128)(2,1)} async-done(((bf16[16,128,1280]{2,1,0:T(8,128)(2,1)}), bf16[16,128,1280]{2,1,0:T(8,128)(2,1)}, u32[]{:S(2)}, u32[]{:S(2)}) %all-to-all-start.1) | async-done | bytes 5242912 | tf_op jit(solution)/shard_map/all_to_all | solution.py:171
  101.5 6.3 %fusion.2 = bf16[1,128,1280]{2,0,1:T(2,128)(2,1)S(1)} fusion(bf16[16,128,1280]{2,1,0:T(8,128)(2,1)} %all-to-all-done.1, s32[]{:T(128)} %bitcast), kind=kOutput, calls=%fused_computation.5 | convolution fusion | flops 5242896 | bytes 5570564 | tf_op jit(solution)/shard_map/qg,qrd->grd/dot_general | solution.py:172
  107.8 0.0 copy-start.3
  107.9 0.8 copy-done.3
  108.7 0.0 copy-done
  108.7 1.9 convolution_convert_fusion.1
  110.6 1.9 copy.36
  112.5 2.7 convolution_convert_fusion.2
  115.2 2.4 fusion.58
  117.6 3.6 convolution_convert_fusion.3
  121.2 3.5 convolution_convert_fusion.4
  124.7 0.0 copy-start.2
  124.7 0.0 copy-start.7
  124.7 0.0 copy-start.8
  124.7 0.0 copy-start.9
  124.7 5.1 %fusion.53 = f32[1280,1280]{0,1:T(8,128)} fusion(bf16[128,1280]{0,1:T(8,128)(2,1)} %bitcast.78, bf16[1,128,1280]{2,0,1:T(2,128)(2,1)} %copy-done.3), kind=kOutput, calls=%fused_computation.82 | convolution fusion | flops 419430400 | bytes 7208960 | tf_op jit(solution)/shard_map/dot_general | solution.py:94
  129.8 0.0 copy-done.2
  129.8 0.0 copy-done.7
  129.9 0.0 copy-done.8
  129.9 0.0 copy-done.9
  129.9 0.0 copy-start.4
  129.9 0.0 copy-start.5
  129.9 7.5 %fusion.54 = (f32[128]{0:T(128)S(1)}, f32[128]{0:T(128)S(1)}, f32[128,1280]{1,0:T(8,128)S(1)}) fusion(f32[128]{0:T(128)S(1)} %add_rsqrt_fusion, f32[128,1280]{1,0:T(8,128)S(1)} %copy-done.2, f32[128]{0:T(128)S(1)} %broadcast_multiply_fusion.2, bf16[1280,3840]{1,0:T(8,128)(2,1)} %param.16, bf16[128,1280]{0,1:T(8,128)(2,1)S(1)} %bitcast.93, ...), kind=kOutput, calls=%fused_computation.83 | convolution fusion | flops 1262059264 | bytes 12126208 | tf_op jit(solution)/shard_map/dot_general | solution.py:103
  137.4 0.0 copy-done.4
  137.4 0.0 copy-done.5
  137.4 3.6 convolution_bitcast_fusion
  141.0 0.0 all-reduce.5.cloned.1.call-update
  141.0 1.8 fusion.8
  142.9 3.5 multiply_convert_fusion.1
  146.4 5.1 %all-to-all-start = ((bf16[16,128,1280]{2,1,0:T(8,128)(2,1)}), bf16[16,128,1280]{2,1,0:T(8,128)(2,1)}, u32[]{:S(2)}, u32[]{:S(2)}) async-start(bf16[16,128,1280]{2,1,0:T(8,128)(2,1)} %multiply_convert_fusion.1), calls=%async_computation | async-start | bytes 10485760 | tf_op jit(solution)/shard_map/all_to_all | solution.py:162
  151.5 88.7 %all-to-all-done = bf16[16,128,1280]{2,1,0:T(8,128)(2,1)} async-done(((bf16[16,128,1280]{2,1,0:T(8,128)(2,1)}), bf16[16,128,1280]{2,1,0:T(8,128)(2,1)}, u32[]{:S(2)}, u32[]{:S(2)}) %all-to-all-start) | async-done | bytes 5242912 | tf_op jit(solution)/shard_map/all_to_all | solution.py:162
  240.1 5.7 %fusion.4 = bf16[1,128,1280]{2,0,1:T(2,128)(2,1)S(1)} fusion(bf16[16,128,1280]{2,1,0:T(8,128)(2,1)} %all-to-all-done, bf16[16]{0:T(256)(128)(2,1)S(1)} %fusion.38), kind=kOutput, calls=%fused_computation.7 | convolution fusion | flops 5242880 | bytes 5570592 | tf_op jit(solution)/shard_map/rm,rid->mid/dot_general | solution.py:163
  245.8 0.8 copy.59
  246.6 2.9 dynamic_update_slice.4
  249.5 124.4 %all-reduce.5.cloned.1.call-done = (f32[1152,1280]{0,1:T(8,128)}, f32[1280,1280]{0,1:T(8,128)}) async-done(((f32[1152,1280]{0,1:T(8,128)}, f32[1280,1280]{0,1:T(8,128)}), (f32[1152,1280]{0,1:T(8,128)}, f32[1280,1280]{0,1:T(8,128)})) %all-reduce.5.cloned.1.call-update) | async-done | bytes 12451856
  373.9 1.5 constant_dynamic-slice_fusion.3
  375.5 1.5 constant_dynamic-slice_fusion.2
  (4 shorter events, 0.0 us)
Async XLA Ops:
  7.2 101.5 %copy-start = (bf16[1280,1280]{1,0:T(8,128)(2,1)S(1)}, bf16[1280,1280]{1,0:T(8,128)(2,1)}, u32[]{:S(2)}) copy-start(bf16[1280,1280]{1,0:T(8,128)(2,1)} %param.17) | copy-start | bytes 9830404
  16.5 85.0 %all-to-all-start.1 = ((bf16[16,128,1280]{2,1,0:T(8,128)(2,1)}), bf16[16,128,1280]{2,1,0:T(8,128)(2,1)}, u32[]{:S(2)}, u32[]{:S(2)}) async-start(bf16[16,128,1280]{2,1,0:T(8,128)(2,1)} %multiply_convert_fusion), calls=%async_computation.1 | async-start | bytes 10485760 | tf_op jit(solution)/shard_map/all_to_all | solution.py:171
  24.2 349.7 %all-reduce.5.cloned.1.call-start = ((), (), s32[]{:S(2)}) async-start(), calls=%async_computation.2 | async-start | bytes 24903680
  26.9 5.6 %copy-start.1 = (f32[128,1280]{1,0:T(8,128)}, f32[128,1280]{1,0:T(8,128)S(1)}, u32[]{:S(2)}) copy-start(f32[128,1280]{1,0:T(8,128)S(1)} %get-tuple-element.37) | copy-start | bytes 1966084
  27.1 11.9 %copy-start.6 = (s32[128,1]{0,1:T(1,128)S(1)}, s32[128,1]{0,1:T(1,128)}, u32[]{:S(2)}) copy-start(s32[128,1]{0,1:T(1,128)} %param.11) | copy-start | bytes 1540
  107.8 0.8 copy-start.3
  124.7 5.1 %copy-start.2 = (f32[128,1280]{1,0:T(8,128)S(1)}, f32[128,1280]{1,0:T(8,128)}, u32[]{:S(2)}) copy-start(f32[128,1280]{1,0:T(8,128)} %copy-done.1) | copy-start | bytes 1966084
  124.7 5.1 %copy-start.7 = (bf16[16,80,128]{2,1,0:T(8,128)(2,1)S(1)}, bf16[16,80,128]{2,1,0:T(8,128)(2,1)}, u32[]{:S(2)}) copy-start(bf16[16,80,128]{2,1,0:T(8,128)(2,1)} %convolution_convert_fusion.2) | copy-start | bytes 983044
  124.7 5.1 %copy-start.8 = (bf16[16,80,128]{2,1,0:T(8,128)(2,1)S(1)}, bf16[16,80,128]{2,1,0:T(8,128)(2,1)}, u32[]{:S(2)}) copy-start(bf16[16,80,128]{2,1,0:T(8,128)(2,1)} %convolution_convert_fusion.3) | copy-start | bytes 983044
  124.7 5.1 %copy-start.9 = (bf16[16,80,128]{2,1,0:T(8,128)(2,1)S(1)}, bf16[16,80,128]{2,1,0:T(8,128)(2,1)}, u32[]{:S(2)}) copy-start(bf16[16,80,128]{2,1,0:T(8,128)(2,1)} %convolution_convert_fusion.4) | copy-start | bytes 983044
  129.9 7.5 %copy-start.4 = (bf16[1,128,1280]{2,0,1:T(2,128)(2,1)S(1)}, bf16[1,128,1280]{2,0,1:T(2,128)(2,1)}, u32[]{:S(2)}) copy-start(bf16[1,128,1280]{2,0,1:T(2,128)(2,1)} %copy-done.3) | copy-start | bytes 983044
  129.9 7.5 %copy-start.5 = (bf16[128,1152]{1,0:T(8,128)(2,1)S(1)}, bf16[128,1152]{1,0:T(8,128)(2,1)}, u32[]{:S(2)}) copy-start(bf16[128,1152]{1,0:T(8,128)(2,1)} %param.9) | copy-start | bytes 884740
  146.4 93.7 %all-to-all-start = ((bf16[16,128,1280]{2,1,0:T(8,128)(2,1)}), bf16[16,128,1280]{2,1,0:T(8,128)(2,1)}, u32[]{:S(2)}, u32[]{:S(2)}) async-start(bf16[16,128,1280]{2,1,0:T(8,128)(2,1)} %multiply_convert_fusion.1), calls=%async_computation | async-start | bytes 10485760 | tf_op jit(solution)/shard_map/all_to_all | solution.py:162
Sparse Core Ops, SparseCore 0:
  141.1 232.7 all-reduce.4
where the time goes:
time: 385 us; the launch traced here: 384 us
  waiting for transfers between devices  268 us (70%)
  matrix products  57.4 us (15%)
  local copies, waits for them, and re-layouts  19.8 us (5%)
  between operations  14.9 us (4%)
  starting transfers between devices  12.7 us (3%)
  other arithmetic  10.6 us (3%)
    unnamed x2, waiting for transfers between devices  124 us
    all_to_all x1, waiting for transfers between devices, shards(): lax.all_to_all(outgoing, 'llm', split_axis=0, concat_axis=0, tiled=True)  88.7 us
    all_to_all x1, waiting for transfers between devices, shards(): lax.all_to_all(grad_sent, 'llm', split_axis=0, concat_axis=0, tiled=True)  55.3 us
  transfers between devices with their start and end apart: 3, of which 3 were waited for; matrix products, arithmetic and copies ran while one was open for 10% of the time, Pallas kernels for 0%

commit v1 on v0

v1 whole, which is shorter than its diff:
```python
import jax
import jax.numpy as jnp
from jax import lax
from jax.experimental import pallas as pl
from jax.experimental.pallas import tpu as pltpu
from jax.sharding import PartitionSpec as P

D = 1280
HEADS = 16
HEAD_DIM = 80
PIN = 1152
ROWS = 128
SEQ = 160
N_LLM = 16
N_ENC = 8
HALF = 640
SCALE = HEAD_DIM ** (-0.5)
PART_COLS = ((0, 384), (384, 256))

BF = jnp.bfloat16
F32 = jnp.float32
MESH = pl.DeviceIdType.MESH
NN = (((1,), (0,)), ((), ()))
NT = (((1,), (1,)), ((), ()))
TN = (((0,), (0,)), ((), ()))


def mm(a, b, dims=NN):
    return lax.dot_general(a, b, dims, preferred_element_type=F32)


def iota(shape, axis):
    return lax.broadcasted_iota(jnp.int32, shape, axis)


def aligned(value, unit):
    return pl.multiple_of(value, unit)


def each(low, high, body):
    def step(i, carry):
        body(i)
        return carry

    lax.fori_loop(low, high, step, 0)


def head_window(j):
    first = 80 * j // 128 * 128
    last = -(-(80 * j + 80) // 128) * 128
    return first, last - first, 80 * j - first


def padded(rows, offset, width):
    pieces = []
    if offset:
        pieces.append(jnp.zeros((offset, ROWS), BF))
    pieces.append(rows)
    if width - offset - 80:
        pieces.append(jnp.zeros((width - offset - 80, ROWS), BF))
    return jnp.concatenate(pieces, axis=0)


def kernel(
    owner_ref, start_ref, seg_hbm, patches_hbm, text_hbm, mgrad_hbm, wp_hbm, wq_hbm, wo_hbm,
    merged_hbm, gpatch_ref, gout_ref,
    seg, pat, text, mgrad, wp, wq, wo,
    perm, sent1, recv1, sent2, emb_in, up, res, nlow, resT, qkv, qkvT, pT, plT, attT, att,
    upT, gaT, gqkvT, gnT, merged, uu, aa, gt, r1, s1, r2, s2, x3, r3,
    local_sem, ex_send, ex_recv, pair_send, pair_recv, p1_send, p1_recv, p2_send, p2_recv,
    p3_send, p3_recv,
):
    llm = lax.axis_index("llm")
    enc = lax.axis_index("enc")
    y, x = llm // 4, llm % 4
    core = enc % 2
    device = llm * N_ENC + enc
    start = start_ref[0, 0]

    def local(source, target, slot):
        return pltpu.make_async_copy(source, target, local_sem.at[slot])

    def remote(source, target, send, recv, to_llm, to_enc):
        return pltpu.make_async_remote_copy(
            src_ref=source, dst_ref=target, send_sem=send, recv_sem=recv,
            device_id=(to_llm, to_enc), device_id_type=MESH,
        )

    load_mgrad = local(mgrad_hbm, mgrad, 0)
    load_pat = local(patches_hbm, pat, 1)
    load_seg = local(seg_hbm.at[device], seg, 2)
    load_wp = local(wp_hbm, wp, 3)
    load_wq = [
        local(wq_hbm.at[:, pl.ds(D * i, D)], wq.at[:, pl.ds(D * i, D)], 4 + i) for i in range(3)
    ]
    load_wo = local(wo_hbm, wo, 7)
    load_text = local(text_hbm, text, 8)
    for load in (load_mgrad, load_pat, load_seg, load_wp, *load_wq, load_wo, load_text):
        load.start()

    barrier = pltpu.get_barrier_semaphore()

    def greet_llm(k):
        pl.semaphore_signal(
            barrier, inc=1, device_id=((llm + k) % N_LLM, enc), device_id_type=MESH
        )

    def greet_enc(k):
        pl.semaphore_signal(
            barrier, inc=1, device_id=(llm, (enc + k) % N_ENC), device_id_type=MESH
        )

    each(1, N_LLM, greet_llm)
    each(1, N_ENC, greet_enc)

    lane = iota((16, 256), 1)
    row = iota((16, 256), 0)

    def owner_rows(s):
        rank = owner_ref[0, s * N_ENC + enc]
        hit = (lane == rank * 16 + row).astype(F32)
        perm[pl.ds(aligned(s * 16, 16), 16), :] = hit.astype(BF)

    each(0, N_LLM, owner_rows)

    load_mgrad.wait()
    take = (iota((ROWS, SEQ), 1) == iota((ROWS, SEQ), 0) + start).astype(F32).astype(BF)
    sent1[0, :, :] = mm(take, mgrad[...]).astype(BF)

    pl.semaphore_wait(barrier, N_LLM - 1 + N_ENC - 1)

    def piece(ref, j):
        return ref.at[pl.ds(aligned(j // 2 * 16, 16), 16), pl.ds(aligned(j % 2 * HALF, 128), HALF)]

    def scatter(way, k):
        to = (llm + k) % N_LLM
        return remote(
            piece(sent1.at[way], to), recv1.at[way, pl.ds(aligned(llm * 16, 16), 16)],
            ex_send.at[way, 0, k], ex_recv.at[way, 0, k], to, enc,
        )

    def scatter_arrival(way, k):
        source = (llm + N_LLM - k) % N_LLM
        return remote(
            piece(sent1.at[way], llm), recv1.at[way, pl.ds(aligned(source * 16, 16), 16)],
            ex_send.at[way, 0, k], ex_recv.at[way, 0, k], (llm + k) % N_LLM, enc,
        )

    def deliver(way, target, k):
        to = (llm + k) % N_LLM
        return remote(
            sent2.at[way, pl.ds(aligned(to * 16, 16), 16)], piece(target, llm),
            ex_send.at[way, 1, k], ex_recv.at[way, 1, k], to, enc,
        )

    def deliver_arrival(way, target, k):
        source = (llm + N_LLM - k) % N_LLM
        return remote(
            sent2.at[way, pl.ds(aligned(llm * 16, 16), 16)], piece(target, source),
            ex_send.at[way, 1, k], ex_recv.at[way, 1, k], (llm + k) % N_LLM, enc,
        )

    def own_piece(ref):
        return ref[pl.ds(aligned(llm // 2 * 16, 16), 16), pl.ds(aligned(llm % 2 * HALF, 128), HALF)]

    def exchange_first(way):
        each(1, N_LLM, lambda k: scatter(way, k).start())
        recv1[way, pl.ds(aligned(llm * 16, 16), 16), :] = own_piece(sent1.at[way])

    def exchange_second(way, target, dims):
        each(1, N_LLM, lambda k: scatter_arrival(way, k).wait_recv())
        sent2[way, :, :] = mm(perm[...], recv1[way], dims).astype(BF)
        each(1, N_LLM, lambda k: deliver(way, target, k).start())
        target[pl.ds(aligned(llm // 2 * 16, 16), 16), pl.ds(aligned(llm % 2 * HALF, 128), HALF)] = (
            sent2[way, pl.ds(aligned(llm * 16, 16), 16), :]
        )

    def exchange_finish(way, target):
        each(1, N_LLM, lambda k: deliver_arrival(way, target, k).wait_recv())

    exchange_first(0)

    other = enc + 1 - 2 * core

    def to_pair(slot, source, target):
        return remote(source, target, pair_send.at[slot], pair_recv.at[slot], llm, other)

    load_pat.wait()
    pair_pat = to_pair(
        0, pat.at[:, pl.ds(aligned((1 - core) * 512, 128), HALF)], aa.at[1, pl.ds(ROWS, ROWS)]
    )
    pair_pat.start()
    aa[1, pl.ds(0, ROWS), :] = pat[:, pl.ds(aligned(core * 512, 128), HALF)]

    load_wp.wait()

    def project(i):
        columns = pl.ds(aligned(i * 256, 256), 256)
        res[:, columns] = mm(pat[...], wp[:, columns])

    each(0, 5, project)
    for i in range(4):
        rows = pl.ds(32 * i, 32)
        values = res[rows, :]
        centred = values - jnp.mean(values, axis=1, keepdims=True)
        inverse = lax.rsqrt(jnp.mean(centred * centred, axis=1, keepdims=True) + 1e-6)
        nlow[rows, :] = (centred * inverse).astype(BF)

    exchange_second(0, up, NN)

    def project_qkv(i):
        columns = pl.ds(aligned(i * 256, 256), 256)
        tile = mm(nlow[...], wq[:, columns]).astype(BF)
        qkv[:, columns] = tile
        qkvT[columns, :] = tile.T

    for i in range(3):
        load_wq[i].wait()
        each(5 * i, 5 * i + 5, project_qkv)

    load_seg.wait()
    one_hot = (iota((8, ROWS), 0) == seg[...]).astype(F32).astype(BF)
    same_image = mm(one_hot, one_hot, TN) > 0.5

    def forward_heads(g):
        base = g * HALF
        for j in range(8):
            first, width, offset = head_window(j)
            head = pl.ds(aligned(base + 80 * j, 16), 80)
            block = pl.ds(aligned((g * 8 + j) * ROWS, ROWS), ROWS)
            keys = qkv[:, pl.ds(aligned(D + base + first, 128), width)]
            scores = mm(keys, padded(qkvT[head, :], offset, width)) * SCALE
            scores = jnp.where(same_image, scores, -1e30)
            weights = jnp.exp(scores - jnp.max(scores, axis=0, keepdims=True))
            probability = weights / jnp.sum(weights, axis=0, keepdims=True)
            low = probability.astype(BF)
            pT[block, :] = probability
            plT[block, :] = low
            values = qkvT[pl.ds(aligned(2 * D + base + 80 * j, 16), 80), :]
            attT[head, :] = mm(values, low).astype(BF)

    each(0, 2, forward_heads)

    def turn_attended(i):
        block = pl.ds(aligned(i * 128, 128), 128)
        att[:, block] = attT[block, :].T

    each(0, 10, turn_attended)
    pair_att = to_pair(
        1, att.at[:, pl.ds(aligned((1 - core) * HALF, 128), HALF)], aa.at[0, pl.ds(ROWS, ROWS)]
    )
    pair_att.start()
    aa[0, pl.ds(0, ROWS), :] = att[:, pl.ds(aligned(core * HALF, 128), HALF)]

    exchange_finish(0, up)

    def turn_upstream(i):
        block = pl.ds(aligned(i * 128, 128), 128)
        upT[block, :] = up[:, block].T

    each(0, 10, turn_upstream)
    pair_up = to_pair(2, upT, uu.at[0, 1])
    pair_up.start()
    uu[0, 0, :, :] = upT[...]

    load_wo.wait()

    def project_out(i):
        columns = pl.ds(aligned(i * 256, 256), 256)
        sent1[1, :, columns] = (res[:, columns] + mm(att[...], wo[:, columns])).astype(BF)

    each(0, 5, project_out)
    exchange_first(1)

    def project_back(i):
        rows = pl.ds(aligned(i * 256, 256), 256)
        gaT[rows, :] = mm(wo[rows, :], upT[...]).astype(BF)

    each(0, 5, project_back)

    def gradient(grad):
        def block(b):
            rows = pl.ds(aligned(b * 80, 16), 80)
            total = mm(uu[grad, 0, rows, :], aa[grad, pl.ds(0, ROWS), :])
            total = total + mm(uu[grad, 1, rows, :], aa[grad, pl.ds(ROWS, ROWS), :])
            gt[grad, b // 4, b % 4] = total.astype(BF)

        each(0, 16, block)

    def first_copy(grad, part, along_y, k):
        first, width = PART_COLS[part]
        columns = pl.ds(first, width)
        if along_y:
            to = (y + k) % 4
            source, to_llm = gt.at[grad, to, :, :, columns], to * 4 + x
        else:
            to = (x + k) % 4
            source, to_llm = gt.at[grad, :, to, :, columns], y * 4 + to
        return remote(
            source, r1.at[grad, k - 1, :, :, columns],
            p1_send.at[grad, part, k - 1], p1_recv.at[grad, part, k - 1], to_llm, enc,
        )

    def second_copy(grad, part, along_y, k):
        first, width = PART_COLS[part]
        columns = pl.ds(first, width)
        if along_y:
            to = (y + k) % 4
            to_llm = to * 4 + x
        else:
            to = (x + k) % 4
            to_llm = y * 4 + to
        return remote(
            s1.at[grad, to, :, columns], r2.at[grad, k - 1, :, columns],
            p2_send.at[grad, part, k - 1], p2_recv.at[grad, part, k - 1], to_llm, enc,
        )

    def third_copy(grad, k):
        to = (enc + k) % N_ENC
        return remote(
            x3.at[grad, pl.ds(aligned(to * 16, 16), 16)], r3.at[grad, k - 1],
            p3_send.at[grad, k - 1], p3_recv.at[grad, k - 1], llm, to,
        )

    def by_core(run):
        @pl.when(core == 0)
        def _():
            run(True)

        @pl.when(core == 1)
        def _():
            run(False)

    def first_phase(grad):
        def run(straight):
            for k in range(1, 4):
                for part in range(2):
                    first_copy(grad, part, straight == (part == 0), k).start()

        by_core(run)

    def second_phase(grad):
        def run(straight):
            for part in range(2):
                first, width = PART_COLS[part]
                columns = pl.ds(first, width)
                along_y = straight == (part == 0)
                for k in range(1, 4):
                    first_copy(grad, part, along_y, k).wait_recv()

                def add(i, part=part, columns=columns, along_y=along_y):
                    own = gt[grad, y, i, :, columns] if along_y else gt[grad, i, x, :, columns]
                    total = own.astype(F32)
                    for k in range(3):
                        total = total + r1[grad, k, i, :, columns].astype(F32)
                    s1[grad, i, :, columns] = total.astype(BF)

                each(0, 4, add)
                for k in range(1, 4):
                    second_copy(grad, part, not along_y, k).start()

        by_core(run)

    def third_phase(grad):
        def run(straight):
            for part in range(2):
                first, width = PART_COLS[part]
                columns = pl.ds(first, width)
                along_y = straight != (part == 0)
                for k in range(1, 4):
                    second_copy(grad, part, along_y, k).wait_recv()
                total = s1[grad, y if along_y else x, :, columns].astype(F32)
                for k in range(3):
                    total = total + r2[grad, k, :, columns].astype(F32)
                s2[:, columns] = total.astype(BF)

        by_core(run)
        spread_row = iota((ROWS, 80), 0)
        spread = jnp.logical_and(
            iota((ROWS, 80), 1) == spread_row // 16 * 10 + spread_row % 16, spread_row % 16 < 10
        )
        x3[grad, :, :] = mm(spread.astype(F32).astype(BF), s2[...]).astype(BF)
        each(1, N_ENC, lambda k: third_copy(grad, k).start())

    def last_phase(grad, out_ref, shift):
        each(1, N_ENC, lambda k: third_copy(grad, k).wait_recv())
        mine = x3[grad, pl.ds(aligned(enc * 16, 16), 16), :].astype(F32)
        for k in (2, 4, 6):
            mine = mine + r3[grad, k - 1].astype(F32)
        theirs = r3[grad, 0].astype(F32)
        for k in (3, 5, 7):
            theirs = theirs + r3[grad, k - 1].astype(F32)
        out_ref[:, pl.ds(aligned(core * shift, 128), HALF)] = mine[:10, :]
        out_ref[:, pl.ds(aligned((1 - core) * shift, 128), HALF)] = theirs[:10, :]

    def finish_sends(grad):
        def run(straight):
            for part in range(2):
                along_y = straight == (part == 0)
                for k in range(1, 4):
                    first_copy(grad, part, along_y, k).wait_send()
                    second_copy(grad, part, not along_y, k).wait_send()

        by_core(run)
        each(1, N_ENC, lambda k: third_copy(grad, k).wait_send())

    pair_att.wait_recv()
    pair_up.wait_recv()
    gradient(0)
    first_phase(0)

    def backward_heads(g):
        base = g * HALF
        for j in range(8):
            first, width, offset = head_window(j)
            head = pl.ds(aligned(base + 80 * j, 16), 80)
            head_k = pl.ds(aligned(D + base + 80 * j, 16), 80)
            head_v = pl.ds(aligned(2 * D + base + 80 * j, 16), 80)
            block = pl.ds(aligned((g * 8 + j) * ROWS, ROWS), ROWS)
            values = qkv[:, pl.ds(aligned(2 * D + base + first, 128), width)]
            rows = gaT[head, :]
            grad_prob = mm(values, padded(rows, offset, width))
            probability = pT[block, :]
            weighted = jnp.sum(grad_prob * probability, axis=0, keepdims=True)
            low = (probability * (grad_prob - weighted) * SCALE).astype(BF)
            gqkvT[head, :] = mm(qkvT[head_k, :], low).astype(BF)
            gqkvT[head_k, :] = mm(qkvT[head, :], low, NT).astype(BF)
            gqkvT[head_v, :] = mm(rows, plT[block, :], NT).astype(BF)

    each(0, 2, backward_heads)

    exchange_second(1, emb_in, TN)
    second_phase(0)

    def turn_residual(i):
        block = pl.ds(aligned(i * 128, 128), 128)
        resT[block, :] = res[:, block].T

    each(0, 10, turn_residual)
    mean = jnp.sum(resT[...], axis=0, keepdims=True) * (1.0 / D)
    centred = resT[...] - mean
    inverse = lax.rsqrt(jnp.sum(centred * centred, axis=0, keepdims=True) * (1.0 / D) + 1e-6)

    def back_qkv(i, carry):
        rows = pl.ds(aligned(i * 256, 256), 256)
        tile = mm(wq[rows, :], gqkvT[...])
        gnT[rows, :] = tile
        normed = (resT[rows, :] - mean) * inverse
        return (
            carry[0] + jnp.sum(tile, axis=0, keepdims=True),
            carry[1] + jnp.sum(tile * normed, axis=0, keepdims=True),
        )

    zero = jnp.zeros((1, ROWS), F32)
    mean_grad, mean_cross = lax.fori_loop(0, 5, back_qkv, (zero, zero))
    mean_grad = mean_grad * (1.0 / D)
    mean_cross = mean_cross * (1.0 / D)

    third_phase(0)

    def residual_grad(i):
        rows = pl.ds(aligned(i * 256, 256), 256)
        normed = (resT[rows, :] - mean) * inverse
        total = upT[rows, :].astype(F32) + inverse * (
            gnT[rows, :] - mean_grad - normed * mean_cross
        )
        uu[1, 0, rows, :] = total.astype(BF)

    each(0, 5, residual_grad)
    pair_res = to_pair(3, uu.at[1, 0], uu.at[1, 1])
    pair_res.start()
    pair_pat.wait_recv()
    pair_res.wait_recv()
    gradient(1)
    first_phase(1)

    exchange_finish(1, emb_in)
    load_text.wait()
    position = iota((SEQ, ROWS), 0)
    put = (position == iota((SEQ, ROWS), 1) + start).astype(F32).astype(BF)

    def merge(i):
        columns = pl.ds(aligned(i * 256, 256), 256)
        placed = mm(put, emb_in[:, columns])
        place = iota((SEQ, 256), 0)
        inside = jnp.logical_and(place >= start, place < start + ROWS)
        merged[:, columns] = jnp.where(inside, placed, text[:, columns].astype(F32)).astype(BF)

    each(0, 5, merge)
    store_merged = local(merged, merged_hbm, 9)
    store_merged.start()
    last_phase(0, gout_ref, HALF)

    second_phase(1)
    third_phase(1)
    last_phase(1, gpatch_ref, 512)

    store_merged.wait()
    for pair in (pair_pat, pair_att, pair_up, pair_res):
        pair.wait_send()

    def finish_exchange(k):
        scatter(0, k).wait_send()
        scatter(1, k).wait_send()
        deliver(0, up, k).wait_send()
        deliver(1, emb_in, k).wait_send()

    each(1, N_LLM, finish_exchange)
    finish_sends(0)
    finish_sends(1)


def shards(
    patches, image_seg, owner_slot, place_start, text_embeds, merged_grad, w_patch, w_qkv, w_out
):
    smem = pl.BlockSpec(memory_space=pltpu.SMEM)
    anywhere = pl.BlockSpec(memory_space=pl.ANY)
    vmem = pl.BlockSpec(memory_space=pltpu.VMEM)
    dma = pltpu.SemaphoreType.DMA
    merged, grad_patch, grad_out = pl.pallas_call(
        kernel,
        out_shape=(
            jax.ShapeDtypeStruct((SEQ, D), BF),
            jax.ShapeDtypeStruct((10, PIN), F32),
            jax.ShapeDtypeStruct((10, D), F32),
        ),
        in_specs=[smem, smem] + [anywhere] * 7,
        out_specs=(anywhere, vmem, vmem),
        scratch_shapes=[
            pltpu.VMEM((1, ROWS), jnp.int32),
            pltpu.VMEM((ROWS, PIN), BF),
            pltpu.VMEM((SEQ, D), BF),
            pltpu.VMEM((SEQ, D), BF),
            pltpu.VMEM((PIN, D), BF),
            pltpu.VMEM((D, 3 * D), BF),
            pltpu.VMEM((D, D), BF),
            pltpu.VMEM((256, 256), BF),
            pltpu.VMEM((2, ROWS, D), BF),
            pltpu.VMEM((2, 256, HALF), BF),
            pltpu.VMEM((2, 256, HALF), BF),
            pltpu.VMEM((ROWS, D), BF),
            pltpu.VMEM((ROWS, D), BF),
            pltpu.VMEM((ROWS, D), F32),
            pltpu.VMEM((ROWS, D), BF),
            pltpu.VMEM((D, ROWS), F32),
            pltpu.VMEM((ROWS, 3 * D), BF),
            pltpu.VMEM((3 * D, ROWS), BF),
            pltpu.VMEM((HEADS * ROWS, ROWS), F32),
            pltpu.VMEM((HEADS * ROWS, ROWS), BF),
            pltpu.VMEM((D, ROWS), BF),
            pltpu.VMEM((ROWS, D), BF),
            pltpu.VMEM((D, ROWS), BF),
            pltpu.VMEM((D, ROWS), BF),
            pltpu.VMEM((3 * D, ROWS), BF),
            pltpu.VMEM((D, ROWS), F32),
            pltpu.VMEM((SEQ, D), BF),
            pltpu.VMEM((2, 2, D, ROWS), BF),
            pltpu.VMEM((2, 2 * ROWS, HALF), BF),
            pltpu.VMEM((2, 4, 4, 80, HALF), BF),
            pltpu.VMEM((2, 3, 4, 80, HALF), BF),
            pltpu.VMEM((2, 4, 80, HALF), BF),
            pltpu.VMEM((2, 3, 80, HALF), BF),
            pltpu.VMEM((80, HALF), BF),
            pltpu.VMEM((2, ROWS, HALF), BF),
            pltpu.VMEM((2, 7, 16, HALF), BF),
            dma((10,)),
            dma((2, 2, N_LLM)),
            dma((2, 2, N_LLM)),
            dma((4,)),
            dma((4,)),
            dma((2, 2, 3)),
            dma((2, 2, 3)),
            dma((2, 2, 3)),
            dma((2, 2, 3)),
            dma((2, 7)),
            dma((2, 7)),
        ],
        compiler_params=pltpu.CompilerParams(
            collective_id=0, has_side_effects=True, vmem_limit_bytes=56 * 1024 * 1024
        ),
    )(
        owner_slot.reshape(1, 128), place_start, image_seg, patches, text_embeds, merged_grad,
        w_patch, w_qkv, w_out,
    )
    return (merged, grad_patch.T, grad_out.T)


def solution(mesh):
    rows = P(("llm", "enc"), None)
    columns = P(None, ("llm", "enc"))
    return jax.shard_map(
        shards,
        mesh=mesh,
        in_specs=(rows, P(), P(), rows, rows, rows, P(), P(), P()),
        out_specs=(rows, columns, columns),
        check_vma=False,
    )
```

time: 385 us -> 85.4 us (0.22)
  waiting for transfers between devices: 268 us -> 0 us
  Pallas kernels: 0 us -> 79 us
  matrix products: 57.4 us -> 0 us
  local copies, waits for them, and re-layouts: 19.8 us -> 4.83 us
  between operations: 14.9 us -> 1.29 us
  starting transfers between devices: 12.7 us -> 0 us
  other arithmetic: 10.6 us -> 0 us
    all_to_all x2 -> x0, waiting for transfers between devices: 144 us -> none  [the longest x1 88.7 us: shards(): lax.all_to_all(outgoing, 'llm', split_axis=0, concat_axis=0, tiled=True)]
    unnamed x2 -> x0, waiting for transfers between devices: 124 us -> none
    pallas_call x0 -> x1, Pallas kernels: none -> 79 us  [shards(): pl.pallas_call(kernel, out_shape=(jax.ShapeDtypeStruct((SEQ, D), BF), jax...]
    dot_general x14 -> x0, matrix products: 54.8 us -> none  [the longest x1 7.48 us: backprop(): lax.dot_general(grad_qkv_low, w_qkv, CONTRACT_COLS, preferred_element_typ...]
    all_to_all x2 -> x0, starting transfers between devices: 12.7 us -> none  [the longest x1 7.63 us: shards(): lax.all_to_all(grad_sent, 'llm', split_axis=0, concat_axis=0, tiled=True)]
    convert_element_type x3 -> x0, other arithmetic: 7.3 us -> none  [the longest x1 3.6 us: shards(): grad_sent = jnp.einsum('rm,mid->rid', arrive_select, slot_grads, preferre...]
    slice x4 -> x0, local copies, waits for them, and re-layouts: 6.57 us -> none  [the longest x2 2.85 us: attention_forward(): keys_all = split_heads(qkv_low[:, :, D:2 * D], blocks, length)]
  transfers between devices with their start and end apart: 3 -> 0, of which waited for: 3 -> 0; matrix products, arithmetic and copies ran while one was open for 10% -> 0% of each run, Pallas kernels for 0% -> 0%
where the time goes in v1:
time: 85.4 us; the launch traced here: 85.1 us
  Pallas kernels  79 us (93%)
  local copies, waits for them, and re-layouts  4.83 us (6%)
  between operations  1.29 us (2%)
    pallas_call x1, Pallas kernels, shards(): pl.pallas_call(kernel, out_shape=(jax.ShapeDtypeStruct((SEQ, D), BF), jax...  79 us
    unnamed x3, local copies, waits for them, and re-layouts  4.83 us

profile of v1, /device:TPU:1, one launch (start us, length us, event | category | flops | bytes accessed | tf_op | source)
XLA Modules:
  0.0 85.1 jit_solution(6029760838523668318)
XLA Ops:
  1.3 79.0 %shard_map.112 = (bf16[160,1280]{1,0:T(8,128)(2,1)}, f32[10,1152]{1,0:T(8,128)}, f32[10,1280]{1,0:T(8,128)}) custom-call(s32[1,128]{1,0:T(1,128)} %bitcast.5, s32[1,1]{1,0:T(1,128)S(6)} %copy.15.start_ref, s32[128,1,128]{2,1,0:T(1,128)} %seg_hbm.1, bf16[128,1152]{1,0:T(8,128)(2,1)} %patches_hbm.1, bf16[160,1280]{1,0:T(8,128)(2,1)} %text_hbm.1, ...), custom_call_target="tpu_custom_call" | custom-call | tf_op jit(solution)/shard_map/pallas_call | solution.py:520
  80.3 1.8 %copy.16 = bf16[160,1280]{1,0:T(8,128)(2,1)} copy(bf16[160,1280]{1,0:T(8,128)(2,1)} %get-tuple-element.12) | data formatting | bytes 819200
  82.1 1.5 %copy.17 = f32[1152,10]{0,1:T(8,128)} copy(f32[1152,10]{0,1:T(8,128)} %bitcast.4) | data formatting | bytes 92160
  83.6 1.5 %copy.18 = f32[1280,10]{0,1:T(8,128)} copy(f32[1280,10]{0,1:T(8,128)} %bitcast.3) | data formatting | bytes 102400

commit v2 on v1

--- a/solution.py
+++ b/solution.py
@@ -15,7 +15,11 @@
 N_ENC = 8
 HALF = 640
 SCALE = HEAD_DIM ** (-0.5)
-PART_COLS = ((0, 384), (384, 256))
+
+OUT_PARTS = ((pl.ds(256, 384), 2), (pl.ds(0, 128), 0), (pl.ds(128, 128), 1))
+OUT_STRAIGHT, OUT_CROSSED = pl.ds(0, 256), pl.ds(256, 384)
+PATCH_PARTS = ((pl.ds(0, 256), 0), (pl.ds(256, 256), 1), (pl.ds(512, 128), 2))
+PATCH_STRAIGHT, PATCH_CROSSED = pl.ds(0, 512), pl.ds(512, 128)
 
 BF = jnp.bfloat16
 F32 = jnp.float32
@@ -63,19 +67,20 @@
 
 def kernel(
     owner_ref, start_ref, seg_hbm, patches_hbm, text_hbm, mgrad_hbm, wp_hbm, wq_hbm, wo_hbm,
-    merged_hbm, gpatch_ref, gout_ref,
+    merged_hbm, gpatch_hbm, gout_hbm,
     seg, pat, text, mgrad, wp, wq, wo,
     perm, sent1, recv1, sent2, emb_in, up, res, nlow, resT, qkv, qkvT, pT, plT, attT, att,
-    upT, gaT, gqkvT, gnT, merged, uu, aa, gt, r1, s1, r2, s2, x3, r3,
+    upT, gaT, gqkvT, gnT, merged, gpatch, gout, uu, aa, gt, r1, s1, r2, x3, r3, r4,
     local_sem, ex_send, ex_recv, pair_send, pair_recv, p1_send, p1_recv, p2_send, p2_recv,
-    p3_send, p3_recv,
+    p3_send, p3_recv, p4_send, p4_recv,
 ):
     llm = lax.axis_index("llm")
     enc = lax.axis_index("enc")
     y, x = llm // 4, llm % 4
-    core = enc % 2
+    z, core = enc // 2, enc % 2
     device = llm * N_ENC + enc
     start = start_ref[0, 0]
+    arrivals, sends = {}, []
 
     def local(source, target, slot):
         return pltpu.make_async_copy(source, target, local_sem.at[slot])
@@ -113,6 +118,16 @@
     each(1, N_LLM, greet_llm)
     each(1, N_ENC, greet_enc)
 
+    def greet_crossed(e):
+        for to_llm, to_enc in ((y * 4 + z, e), (y * 4 + e // 2, x * 2 + e % 2)):
+            @pl.when(jnp.logical_or(to_llm != llm, to_enc != enc))
+            def _(to_llm=to_llm, to_enc=to_enc):
+                pl.semaphore_signal(
+                    barrier, inc=1, device_id=(to_llm, to_enc), device_id_type=MESH
+                )
+
+    each(0, N_ENC, greet_crossed)
+
     lane = iota((16, 256), 1)
     row = iota((16, 256), 0)
 
@@ -127,7 +142,7 @@
     take = (iota((ROWS, SEQ), 1) == iota((ROWS, SEQ), 0) + start).astype(F32).astype(BF)
     sent1[0, :, :] = mm(take, mgrad[...]).astype(BF)
 
-    pl.semaphore_wait(barrier, N_LLM - 1 + N_ENC - 1)
+    pl.semaphore_wait(barrier, N_LLM - 1 + 3 * N_ENC - 1 - 2 * (x == z).astype(jnp.int32))
 
     def piece(ref, j):
         return ref.at[pl.ds(aligned(j // 2 * 16, 16), 16), pl.ds(aligned(j % 2 * HALF, 128), HALF)]
@@ -165,31 +180,38 @@
 
     def exchange_first(way):
         each(1, N_LLM, lambda k: scatter(way, k).start())
+        arrivals["scatter", way] = lambda: each(
+            1, N_LLM, lambda k: scatter_arrival(way, k).wait_recv()
+        )
+        sends.append(lambda: each(1, N_LLM, lambda k: scatter(way, k).wait_send()))
         recv1[way, pl.ds(aligned(llm * 16, 16), 16), :] = own_piece(sent1.at[way])
 
     def exchange_second(way, target, dims):
-        each(1, N_LLM, lambda k: scatter_arrival(way, k).wait_recv())
+        arrivals.pop(("scatter", way))()
         sent2[way, :, :] = mm(perm[...], recv1[way], dims).astype(BF)
         each(1, N_LLM, lambda k: deliver(way, target, k).start())
+        arrivals["deliver", way] = lambda: each(
+            1, N_LLM, lambda k: deliver_arrival(way, target, k).wait_recv()
+        )
+        sends.append(lambda: each(1, N_LLM, lambda k: deliver(way, target, k).wait_send()))
         target[pl.ds(aligned(llm // 2 * 16, 16), 16), pl.ds(aligned(llm % 2 * HALF, 128), HALF)] = (
             sent2[way, pl.ds(aligned(llm * 16, 16), 16), :]
         )
 
-    def exchange_finish(way, target):
-        each(1, N_LLM, lambda k: deliver_arrival(way, target, k).wait_recv())
-
     exchange_first(0)
 
     other = enc + 1 - 2 * core
 
     def to_pair(slot, source, target):
-        return remote(source, target, pair_send.at[slot], pair_recv.at[slot], llm, other)
+        copy = remote(source, target, pair_send.at[slot], pair_recv.at[slot], llm, other)
+        copy.start()
+        arrivals["pair", slot] = copy.wait_recv
+        sends.append(copy.wait_send)
 
     load_pat.wait()
-    pair_pat = to_pair(
+    to_pair(
         0, pat.at[:, pl.ds(aligned((1 - core) * 512, 128), HALF)], aa.at[1, pl.ds(ROWS, ROWS)]
     )
-    pair_pat.start()
     aa[1, pl.ds(0, ROWS), :] = pat[:, pl.ds(aligned(core * 512, 128), HALF)]
 
     load_wp.wait()
@@ -246,22 +268,20 @@
         att[:, block] = attT[block, :].T
 
     each(0, 10, turn_attended)
-    pair_att = to_pair(
+    to_pair(
         1, att.at[:, pl.ds(aligned((1 - core) * HALF, 128), HALF)], aa.at[0, pl.ds(ROWS, ROWS)]
     )
-    pair_att.start()
     aa[0, pl.ds(0, ROWS), :] = att[:, pl.ds(aligned(core * HALF, 128), HALF)]
 
-    exchange_finish(0, up)
+    arrivals.pop(("deliver", 0))()
 
     def turn_upstream(i):
         block = pl.ds(aligned(i * 128, 128), 128)
         upT[block, :] = up[:, block].T
 
     each(0, 10, turn_upstream)
-    pair_up = to_pair(2, upT, uu.at[0, 1])
-    pair_up.start()
-    uu[0, 0, :, :] = upT[...]
+    to_pair(2, upT, uu.at[0, :, pl.ds(ROWS, ROWS)])
+    uu[0, :, pl.ds(0, ROWS)] = upT[...]
 
     load_wo.wait()
 
@@ -278,136 +298,169 @@
 
     each(0, 5, project_back)
 
-    def gradient(grad):
+    def gradient(grad, part):
+        columns, _ = part
+
         def block(b):
-            rows = pl.ds(aligned(b * 80, 16), 80)
-            total = mm(uu[grad, 0, rows, :], aa[grad, pl.ds(0, ROWS), :])
-            total = total + mm(uu[grad, 1, rows, :], aa[grad, pl.ds(ROWS, ROWS), :])
-            gt[grad, b // 4, b % 4] = total.astype(BF)
-
-        each(0, 16, block)
-
-    def first_copy(grad, part, along_y, k):
-        first, width = PART_COLS[part]
-        columns = pl.ds(first, width)
-        if along_y:
+            rows = pl.ds(aligned(b * 320, 16), 320)
+            total = mm(uu[grad, rows, :], aa[grad, :, columns])
+            gt[grad, b, :, :, columns] = total.astype(BF).reshape(4, 80, columns.size)
+
+        each(0, 4, block)
+
+    def first_copy(grad, part, k):
+        columns, kind = part
+        if kind == 0:
             to = (y + k) % 4
-            source, to_llm = gt.at[grad, to, :, :, columns], to * 4 + x
+            source, to_llm, to_enc = gt.at[grad, to, :, :, columns], to * 4 + x, enc
+        elif kind == 1:
+            to = (x + k) % 4
+            source, to_llm, to_enc = gt.at[grad, :, to, :, columns], y * 4 + to, enc
         else:
+            to = (z + k) % 4
+            source, to_llm, to_enc = gt.at[grad, :, to, :, columns], llm, to * 2 + core
+        return remote(
+            source, r1.at[grad, k - 1, :, :, columns],
+            p1_send.at[grad, kind, k - 1], p1_recv.at[grad, kind, k - 1], to_llm, to_enc,
+        )
+
+    def second_copy(grad, part, k):
+        columns, kind = part
+        if kind == 0:
             to = (x + k) % 4
-            source, to_llm = gt.at[grad, :, to, :, columns], y * 4 + to
-        return remote(
-            source, r1.at[grad, k - 1, :, :, columns],
-            p1_send.at[grad, part, k - 1], p1_recv.at[grad, part, k - 1], to_llm, enc,
-        )
-
-    def second_copy(grad, part, along_y, k):
-        first, width = PART_COLS[part]
-        columns = pl.ds(first, width)
-        if along_y:
+            to_llm = y * 4 + to
+        else:
             to = (y + k) % 4
             to_llm = to * 4 + x
-        else:
-            to = (x + k) % 4
-            to_llm = y * 4 + to
         return remote(
             s1.at[grad, to, :, columns], r2.at[grad, k - 1, :, columns],
-            p2_send.at[grad, part, k - 1], p2_recv.at[grad, part, k - 1], to_llm, enc,
-        )
-
-    def third_copy(grad, k):
+            p2_send.at[grad, kind, k - 1], p2_recv.at[grad, kind, k - 1], to_llm, enc,
+        )
+
+    def third_copy(grad, columns, k):
         to = (enc + k) % N_ENC
         return remote(
-            x3.at[grad, pl.ds(aligned(to * 16, 16), 16)], r3.at[grad, k - 1],
+            x3.at[grad, pl.ds(aligned(to * 16, 16), 16), columns], r3.at[grad, k - 1, :, columns],
             p3_send.at[grad, k - 1], p3_recv.at[grad, k - 1], llm, to,
         )
 
-    def by_core(run):
-        @pl.when(core == 0)
+    def cross_copy(grad, columns, e):
+        slot = x * 2 + core
+        return remote(
+            x3.at[grad, pl.ds(aligned(e * 16, 16), 16), columns], r4.at[grad, slot, :, columns],
+            p4_send.at[grad, e], p4_recv.at[grad, slot], y * 4 + z, e,
+        )
+
+    def cross_arrival(grad, columns, slot):
+        return remote(
+            x3.at[grad, pl.ds(0, 16), columns], r4.at[grad, slot, :, columns],
+            p4_send.at[grad, 0], p4_recv.at[grad, slot], y * 4 + z, enc,
+        )
+
+    def first_phase(grad, part):
+        _, kind = part
+        for k in range(1, 4):
+            first_copy(grad, part, k).start()
+        arrivals["first", grad, kind] = lambda: [
+            first_copy(grad, part, k).wait_recv() for k in range(1, 4)
+        ]
+        sends.append(lambda: [first_copy(grad, part, k).wait_send() for k in range(1, 4)])
+
+    def second_phase(grad, part):
+        columns, kind = part
+        arrivals.pop(("first", grad, kind))()
+
+        def add(i):
+            if kind == 0:
+                own = gt[grad, y, i, :, columns]
+            else:
+                own = gt[grad, i, x if kind == 1 else z, :, columns]
+            total = own.astype(F32)
+            for k in range(3):
+                total = total + r1[grad, k, i, :, columns].astype(F32)
+            s1[grad, i, :, columns] = total.astype(BF)
+
+        each(0, 4, add)
+        for k in range(1, 4):
+            second_copy(grad, part, k).start()
+        arrivals["second", grad, kind] = lambda: [
+            second_copy(grad, part, k).wait_recv() for k in range(1, 4)
+        ]
+        sends.append(lambda: [second_copy(grad, part, k).wait_send() for k in range(1, 4)])
+
+    spread_row = iota((ROWS, 80), 0)
+    spread = jnp.logical_and(
+        iota((ROWS, 80), 1) == spread_row // 16 * 10 + spread_row % 16, spread_row % 16 < 10
+    )
+    spread = spread.astype(F32).astype(BF)
+
+    def third_sum(grad, part):
+        columns, kind = part
+        arrivals.pop(("second", grad, kind))()
+        total = s1[grad, x if kind == 0 else y, :, columns].astype(F32)
+        for k in range(3):
+            total = total + r2[grad, k, :, columns].astype(F32)
+        x3[grad, :, columns] = mm(spread, total.astype(BF)).astype(BF)
+
+    def third_phase(grad, straight, crossed):
+        each(1, N_ENC, lambda k: third_copy(grad, straight, k).start())
+
+        def send(e):
+            @pl.when(jnp.logical_or(x != z, e != enc))
+            def _():
+                cross_copy(grad, crossed, e).start()
+
+        each(0, N_ENC, send)
+
+        @pl.when(x == z)
         def _():
-            run(True)
-
-        @pl.when(core == 1)
-        def _():
-            run(False)
-
-    def first_phase(grad):
-        def run(straight):
-            for k in range(1, 4):
-                for part in range(2):
-                    first_copy(grad, part, straight == (part == 0), k).start()
-
-        by_core(run)
-
-    def second_phase(grad):
-        def run(straight):
-            for part in range(2):
-                first, width = PART_COLS[part]
-                columns = pl.ds(first, width)
-                along_y = straight == (part == 0)
-                for k in range(1, 4):
-                    first_copy(grad, part, along_y, k).wait_recv()
-
-                def add(i, part=part, columns=columns, along_y=along_y):
-                    own = gt[grad, y, i, :, columns] if along_y else gt[grad, i, x, :, columns]
-                    total = own.astype(F32)
-                    for k in range(3):
-                        total = total + r1[grad, k, i, :, columns].astype(F32)
-                    s1[grad, i, :, columns] = total.astype(BF)
-
-                each(0, 4, add)
-                for k in range(1, 4):
-                    second_copy(grad, part, not along_y, k).start()
-
-        by_core(run)
-
-    def third_phase(grad):
-        def run(straight):
-            for part in range(2):
-                first, width = PART_COLS[part]
-                columns = pl.ds(first, width)
-                along_y = straight != (part == 0)
-                for k in range(1, 4):
-                    second_copy(grad, part, along_y, k).wait_recv()
-                total = s1[grad, y if along_y else x, :, columns].astype(F32)
-                for k in range(3):
-                    total = total + r2[grad, k, :, columns].astype(F32)
-                s2[:, columns] = total.astype(BF)
-
-        by_core(run)
-        spread_row = iota((ROWS, 80), 0)
-        spread = jnp.logical_and(
-            iota((ROWS, 80), 1) == spread_row // 16 * 10 + spread_row % 16, spread_row % 16 < 10
-        )
-        x3[grad, :, :] = mm(spread.astype(F32).astype(BF), s2[...]).astype(BF)
-        each(1, N_ENC, lambda k: third_copy(grad, k).start())
-
-    def last_phase(grad, out_ref, shift):
-        each(1, N_ENC, lambda k: third_copy(grad, k).wait_recv())
-        mine = x3[grad, pl.ds(aligned(enc * 16, 16), 16), :].astype(F32)
+            r4[grad, pl.ds(x * 2 + core, 1), :, crossed] = x3[
+                grad, pl.ds(aligned(enc * 16, 16), 16), crossed
+            ].reshape(1, 16, crossed.size)
+
+        def wait(slot):
+            @pl.when(jnp.logical_or(x != z, slot != x * 2 + core))
+            def _():
+                cross_arrival(grad, crossed, slot).wait_recv()
+
+        def left(e):
+            @pl.when(jnp.logical_or(x != z, e != enc))
+            def _():
+                cross_copy(grad, crossed, e).wait_send()
+
+        def arrived():
+            each(1, N_ENC, lambda k: third_copy(grad, straight, k).wait_recv())
+            each(0, N_ENC, wait)
+
+        def sent():
+            each(1, N_ENC, lambda k: third_copy(grad, straight, k).wait_send())
+            each(0, N_ENC, left)
+
+        arrivals["third", grad] = arrived
+        sends.append(sent)
+
+    def last_phase(grad, total, shift, straight, crossed):
+        arrivals.pop(("third", grad))()
+        mine = x3[grad, pl.ds(aligned(enc * 16, 16), 16), straight].astype(F32)
         for k in (2, 4, 6):
-            mine = mine + r3[grad, k - 1].astype(F32)
-        theirs = r3[grad, 0].astype(F32)
+            mine = mine + r3[grad, k - 1, :, straight].astype(F32)
+        theirs = r3[grad, 0, :, straight].astype(F32)
         for k in (3, 5, 7):
-            theirs = theirs + r3[grad, k - 1].astype(F32)
-        out_ref[:, pl.ds(aligned(core * shift, 128), HALF)] = mine[:10, :]
-        out_ref[:, pl.ds(aligned((1 - core) * shift, 128), HALF)] = theirs[:10, :]
-
-    def finish_sends(grad):
-        def run(straight):
-            for part in range(2):
-                along_y = straight == (part == 0)
-                for k in range(1, 4):
-                    first_copy(grad, part, along_y, k).wait_send()
-                    second_copy(grad, part, not along_y, k).wait_send()
-
-        by_core(run)
-        each(1, N_ENC, lambda k: third_copy(grad, k).wait_send())
-
-    pair_att.wait_recv()
-    pair_up.wait_recv()
-    gradient(0)
-    first_phase(0)
+            theirs = theirs + r3[grad, k - 1, :, straight].astype(F32)
+        for half, value in ((core, mine), (1 - core, theirs)):
+            lanes = pl.ds(aligned(half * shift + straight.start, 128), straight.size)
+            total[:, lanes] = value[:10, :]
+        for half in range(2):
+            value = r4[grad, half, :, crossed].astype(F32)
+            for other_x in range(1, 4):
+                value = value + r4[grad, other_x * 2 + half, :, crossed].astype(F32)
+            total[:, pl.ds(half * shift + crossed.start, crossed.size)] = value[:10, :]
+
+    arrivals.pop(("pair", 1))()
+    arrivals.pop(("pair", 2))()
+    for part in OUT_PARTS:
+        gradient(0, part)
+        first_phase(0, part)
 
     def backward_heads(g):
         base = g * HALF
@@ -430,7 +483,6 @@
     each(0, 2, backward_heads)
 
     exchange_second(1, emb_in, TN)
-    second_phase(0)
 
     def turn_residual(i):
         block = pl.ds(aligned(i * 128, 128), 128)
@@ -456,7 +508,8 @@
     mean_grad = mean_grad * (1.0 / D)
     mean_cross = mean_cross * (1.0 / D)
 
-    third_phase(0)
+    for part in OUT_PARTS[1:] + OUT_PARTS[:1]:
+        second_phase(0, part)
 
     def residual_grad(i):
         rows = pl.ds(aligned(i * 256, 256), 256)
@@ -464,17 +517,20 @@
         total = upT[rows, :].astype(F32) + inverse * (
             gnT[rows, :] - mean_grad - normed * mean_cross
         )
-        uu[1, 0, rows, :] = total.astype(BF)
+        uu[1, rows, pl.ds(0, ROWS)] = total.astype(BF)
 
     each(0, 5, residual_grad)
-    pair_res = to_pair(3, uu.at[1, 0], uu.at[1, 1])
-    pair_res.start()
-    pair_pat.wait_recv()
-    pair_res.wait_recv()
-    gradient(1)
-    first_phase(1)
-
-    exchange_finish(1, emb_in)
+    to_pair(3, uu.at[1, :, pl.ds(0, ROWS)], uu.at[1, :, pl.ds(ROWS, ROWS)])
+    for part in OUT_PARTS:
+        third_sum(0, part)
+    third_phase(0, OUT_STRAIGHT, OUT_CROSSED)
+    arrivals.pop(("pair", 0))()
+    arrivals.pop(("pair", 3))()
+    for part in PATCH_PARTS:
+        gradient(1, part)
+        first_phase(1, part)
+
+    arrivals.pop(("deliver", 1))()
     load_text.wait()
     position = iota((SEQ, ROWS), 0)
     put = (position == iota((SEQ, ROWS), 1) + start).astype(F32).astype(BF)
@@ -489,25 +545,35 @@
     each(0, 5, merge)
     store_merged = local(merged, merged_hbm, 9)
     store_merged.start()
-    last_phase(0, gout_ref, HALF)
-
-    second_phase(1)
-    third_phase(1)
-    last_phase(1, gpatch_ref, 512)
-
+    last_phase(0, gout, HALF, OUT_STRAIGHT, OUT_CROSSED)
+    store_gout = local(gout, gout_hbm, 10)
+    store_gout.start()
+
+    for part in PATCH_PARTS:
+        second_phase(1, part)
+    for part in PATCH_PARTS:
+        third_sum(1, part)
+    third_phase(1, PATCH_STRAIGHT, PATCH_CROSSED)
+    last_phase(1, gpatch, 512, PATCH_STRAIGHT, PATCH_CROSSED)
+    store_gpatch = local(gpatch, gpatch_hbm, 11)
+    store_gpatch.start()
+
+    for sent in sends:
+        sent()
     store_merged.wait()
-    for pair in (pair_pat, pair_att, pair_up, pair_res):
-        pair.wait_send()
-
-    def finish_exchange(k):
-        scatter(0, k).wait_send()
-        scatter(1, k).wait_send()
-        deliver(0, up, k).wait_send()
-        deliver(1, emb_in, k).wait_send()
-
-    each(1, N_LLM, finish_exchange)
-    finish_sends(0)
-    finish_sends(1)
+    store_gout.wait()
+    store_gpatch.wait()
+
+
+def finish_kernel(a, b, c, a_out, b_out, c_out, sem):
+    copies = [
+        pltpu.make_async_copy(source, target, sem.at[i])
+        for i, (source, target) in enumerate(((a, a_out), (b, b_out), (c, c_out)))
+    ]
+    for copy in copies:
+        copy.start()
+    for copy in copies:
+        copy.wait()
 
 
 def shards(
@@ -515,7 +581,6 @@
 ):
     smem = pl.BlockSpec(memory_space=pltpu.SMEM)
     anywhere = pl.BlockSpec(memory_space=pl.ANY)
-    vmem = pl.BlockSpec(memory_space=pltpu.VMEM)
     dma = pltpu.SemaphoreType.DMA
     merged, grad_patch, grad_out = pl.pallas_call(
         kernel,
@@ -525,7 +590,7 @@
             jax.ShapeDtypeStruct((10, D), F32),
         ),
         in_specs=[smem, smem] + [anywhere] * 7,
-        out_specs=(anywhere, vmem, vmem),
+        out_specs=(anywhere, anywhere, anywhere),
         scratch_shapes=[
             pltpu.VMEM((1, ROWS), jnp.int32),
             pltpu.VMEM((ROWS, PIN), BF),
@@ -554,26 +619,30 @@
             pltpu.VMEM((3 * D, ROWS), BF),
             pltpu.VMEM((D, ROWS), F32),
             pltpu.VMEM((SEQ, D), BF),
-            pltpu.VMEM((2, 2, D, ROWS), BF),
+            pltpu.VMEM((10, PIN), F32),
+            pltpu.VMEM((10, D), F32),
+            pltpu.VMEM((2, D, 2 * ROWS), BF),
             pltpu.VMEM((2, 2 * ROWS, HALF), BF),
             pltpu.VMEM((2, 4, 4, 80, HALF), BF),
             pltpu.VMEM((2, 3, 4, 80, HALF), BF),
             pltpu.VMEM((2, 4, 80, HALF), BF),
             pltpu.VMEM((2, 3, 80, HALF), BF),
-            pltpu.VMEM((80, HALF), BF),
             pltpu.VMEM((2, ROWS, HALF), BF),
             pltpu.VMEM((2, 7, 16, HALF), BF),
-            dma((10,)),
+            pltpu.VMEM((2, 8, 16, HALF), BF),
+            dma((12,)),
             dma((2, 2, N_LLM)),
             dma((2, 2, N_LLM)),
             dma((4,)),
             dma((4,)),
-            dma((2, 2, 3)),
-            dma((2, 2, 3)),
-            dma((2, 2, 3)),
-            dma((2, 2, 3)),
+            dma((2, 3, 3)),
+            dma((2, 3, 3)),
+            dma((2, 3, 3)),
+            dma((2, 3, 3)),
             dma((2, 7)),
             dma((2, 7)),
+            dma((2, 8)),
+            dma((2, 8)),
         ],
         compiler_params=pltpu.CompilerParams(
             collective_id=0, has_side_effects=True, vmem_limit_bytes=56 * 1024 * 1024
@@ -582,6 +651,17 @@
         owner_slot.reshape(1, 128), place_start, image_seg, patches, text_embeds, merged_grad,
         w_patch, w_qkv, w_out,
     )
+    merged, grad_patch, grad_out = pl.pallas_call(
+        finish_kernel,
+        out_shape=(
+            jax.ShapeDtypeStruct((SEQ, D), BF),
+            jax.ShapeDtypeStruct((10, PIN), F32),
+            jax.ShapeDtypeStruct((10, D), F32),
+        ),
+        in_specs=[anywhere] * 3,
+        out_specs=(anywhere, anywhere, anywhere),
+        scratch_shapes=[dma((3,))],
+    )(merged, grad_patch, grad_out)
     return (merged, grad_patch.T, grad_out.T)
 
 

time: 85.4 us -> 91.1 us (1.067)
  Pallas kernels: 79 us -> 89.7 us
  local copies, waits for them, and re-layouts: 4.83 us -> 0 us
    pallas_call x0 -> x1, Pallas kernels: none -> 18.3 us  [shards(): pl.pallas_call(finish_kernel, out_shape=(jax.ShapeDtypeStruct((SEQ, D), B...]
    pallas_call x1, Pallas kernels: 79 us -> 71.4 us  [shards(): pl.pallas_call(kernel, out_shape=(jax.ShapeDtypeStruct((SEQ, D), BF), jax...]
    unnamed x3 -> x0, local copies, waits for them, and re-layouts: 4.83 us -> none
where the time goes in v2:
time: 91.1 us; the launch traced here: 91 us
  Pallas kernels  89.7 us (98%)
  between operations  1.29 us (1%)
    pallas_call x1, Pallas kernels, shards(): pl.pallas_call(kernel, out_shape=(jax.ShapeDtypeStruct((SEQ, D), BF), jax...  71.4 us
    pallas_call x1, Pallas kernels, shards(): pl.pallas_call(finish_kernel, out_shape=(jax.ShapeDtypeStruct((SEQ, D), B...  18.3 us

profile of v2, /device:TPU:1, one launch (start us, length us, event | category | flops | bytes accessed | tf_op | source)
XLA Modules:
  0.0 91.0 jit_solution(17313489958162894646)
XLA Ops:
  1.3 71.4 %shard_map.112 = (bf16[160,1280]{1,0:T(8,128)(2,1)}, f32[10,1152]{1,0:T(8,128)}, f32[10,1280]{1,0:T(8,128)}) custom-call(s32[1,128]{1,0:T(1,128)} %bitcast.3, s32[1,1]{1,0:T(1,128)S(6)} %copy.12.start_ref, s32[128,1,128]{2,1,0:T(1,128)} %seg_hbm.1, bf16[128,1152]{1,0:T(8,128)(2,1)} %patches_hbm.1, bf16[160,1280]{1,0:T(8,128)(2,1)} %text_hbm.1, ...), custom_call_target="tpu_custom_call" | custom-call | tf_op jit(solution)/shard_map/pallas_call | solution.py:585
  72.7 18.3 %shard_map.113 = (bf16[160,1280]{1,0:T(8,128)(2,1)}, f32[10,1152]{1,0:T(8,128)}, f32[10,1280]{1,0:T(8,128)}) custom-call(bf16[160,1280]{1,0:T(8,128)(2,1)} %get-tuple-element.9.a, f32[10,1152]{1,0:T(8,128)} %get-tuple-element.10.b, f32[10,1280]{1,0:T(8,128)} %get-tuple-element.11.c), custom_call_target="tpu_custom_call" | custom-call | tf_op jit(solution)/shard_map/pallas_call | solution.py:654

commit v3 on v2

--- a/solution.py
+++ b/solution.py
@@ -17,9 +17,7 @@
 SCALE = HEAD_DIM ** (-0.5)
 
 OUT_PARTS = ((pl.ds(256, 384), 2), (pl.ds(0, 128), 0), (pl.ds(128, 128), 1))
-OUT_STRAIGHT, OUT_CROSSED = pl.ds(0, 256), pl.ds(256, 384)
 PATCH_PARTS = ((pl.ds(0, 256), 0), (pl.ds(256, 256), 1), (pl.ds(512, 128), 2))
-PATCH_STRAIGHT, PATCH_CROSSED = pl.ds(0, 512), pl.ds(512, 128)
 
 BF = jnp.bfloat16
 F32 = jnp.float32
@@ -70,7 +68,7 @@
     merged_hbm, gpatch_hbm, gout_hbm,
     seg, pat, text, mgrad, wp, wq, wo,
     perm, sent1, recv1, sent2, emb_in, up, res, nlow, resT, qkv, qkvT, pT, plT, attT, att,
-    upT, gaT, gqkvT, gnT, merged, gpatch, gout, uu, aa, gt, r1, s1, r2, x3, r3, r4,
+    upT, gaT, gqkvT, gnT, merged, gpatch, gout, uu, aa, gt, r1, s1, r2, crossing, s2, x3, r3,
     local_sem, ex_send, ex_recv, pair_send, pair_recv, p1_send, p1_recv, p2_send, p2_recv,
     p3_send, p3_recv, p4_send, p4_recv,
 ):
@@ -118,15 +116,11 @@
     each(1, N_LLM, greet_llm)
     each(1, N_ENC, greet_enc)
 
-    def greet_crossed(e):
-        for to_llm, to_enc in ((y * 4 + z, e), (y * 4 + e // 2, x * 2 + e % 2)):
-            @pl.when(jnp.logical_or(to_llm != llm, to_enc != enc))
-            def _(to_llm=to_llm, to_enc=to_enc):
-                pl.semaphore_signal(
-                    barrier, inc=1, device_id=(to_llm, to_enc), device_id_type=MESH
-                )
-
-    each(0, N_ENC, greet_crossed)
+    @pl.when(x != z)
+    def _():
+        pl.semaphore_signal(
+            barrier, inc=1, device_id=(y * 4 + z, x * 2 + core), device_id_type=MESH
+        )
 
     lane = iota((16, 256), 1)
     row = iota((16, 256), 0)
@@ -142,7 +136,7 @@
     take = (iota((ROWS, SEQ), 1) == iota((ROWS, SEQ), 0) + start).astype(F32).astype(BF)
     sent1[0, :, :] = mm(take, mgrad[...]).astype(BF)
 
-    pl.semaphore_wait(barrier, N_LLM - 1 + 3 * N_ENC - 1 - 2 * (x == z).astype(jnp.int32))
+    pl.semaphore_wait(barrier, N_LLM - 1 + N_ENC - 1 + (x != z).astype(jnp.int32))
 
     def piece(ref, j):
         return ref.at[pl.ds(aligned(j // 2 * 16, 16), 16), pl.ds(aligned(j % 2 * HALF, 128), HALF)]
@@ -228,7 +222,14 @@
         inverse = lax.rsqrt(jnp.mean(centred * centred, axis=1, keepdims=True) + 1e-6)
         nlow[rows, :] = (centred * inverse).astype(BF)
 
-    exchange_second(0, up, NN)
+    def turn_residual(i):
+        block = pl.ds(aligned(i * 128, 128), 128)
+        resT[block, :] = res[:, block].T
+
+    each(0, 10, turn_residual)
+    mean = jnp.sum(resT[...], axis=0, keepdims=True) * (1.0 / D)
+    centred = resT[...] - mean
+    inverse = lax.rsqrt(jnp.sum(centred * centred, axis=0, keepdims=True) * (1.0 / D) + 1e-6)
 
     def project_qkv(i):
         columns = pl.ds(aligned(i * 256, 256), 256)
@@ -239,6 +240,8 @@
     for i in range(3):
         load_wq[i].wait()
         each(5 * i, 5 * i + 5, project_qkv)
+
+    exchange_second(0, up, NN)
 
     load_seg.wait()
     one_hot = (iota((8, ROWS), 0) == seg[...]).astype(F32).astype(BF)
@@ -337,24 +340,18 @@
             p2_send.at[grad, kind, k - 1], p2_recv.at[grad, kind, k - 1], to_llm, enc,
         )
 
-    def third_copy(grad, columns, k):
+    def cross_copy(grad, part):
+        columns, _ = part
+        return remote(
+            crossing.at[grad, :, columns], s2.at[grad, :, columns],
+            p4_send.at[grad], p4_recv.at[grad], y * 4 + z, x * 2 + core,
+        )
+
+    def third_copy(grad, k):
         to = (enc + k) % N_ENC
         return remote(
-            x3.at[grad, pl.ds(aligned(to * 16, 16), 16), columns], r3.at[grad, k - 1, :, columns],
+            x3.at[grad, pl.ds(aligned(to * 16, 16), 16)], r3.at[grad, k - 1],
             p3_send.at[grad, k - 1], p3_recv.at[grad, k - 1], llm, to,
-        )
-
-    def cross_copy(grad, columns, e):
-        slot = x * 2 + core
-        return remote(
-            x3.at[grad, pl.ds(aligned(e * 16, 16), 16), columns], r4.at[grad, slot, :, columns],
-            p4_send.at[grad, e], p4_recv.at[grad, slot], y * 4 + z, e,
-        )
-
-    def cross_arrival(grad, columns, slot):
-        return remote(
-            x3.at[grad, pl.ds(0, 16), columns], r4.at[grad, slot, :, columns],
-            p4_send.at[grad, 0], p4_recv.at[grad, slot], y * 4 + z, enc,
         )
 
     def first_phase(grad, part):
@@ -400,61 +397,42 @@
         total = s1[grad, x if kind == 0 else y, :, columns].astype(F32)
         for k in range(3):
             total = total + r2[grad, k, :, columns].astype(F32)
-        x3[grad, :, columns] = mm(spread, total.astype(BF)).astype(BF)
-
-    def third_phase(grad, straight, crossed):
-        each(1, N_ENC, lambda k: third_copy(grad, straight, k).start())
-
-        def send(e):
-            @pl.when(jnp.logical_or(x != z, e != enc))
-            def _():
-                cross_copy(grad, crossed, e).start()
-
-        each(0, N_ENC, send)
+        if kind < 2:
+            s2[grad, :, columns] = total.astype(BF)
+            return
+
+        crossing[grad, :, columns] = total.astype(BF)
+
+        def if_other(run):
+            pl.when(x != z)(run)
 
         @pl.when(x == z)
         def _():
-            r4[grad, pl.ds(x * 2 + core, 1), :, crossed] = x3[
-                grad, pl.ds(aligned(enc * 16, 16), 16), crossed
-            ].reshape(1, 16, crossed.size)
-
-        def wait(slot):
-            @pl.when(jnp.logical_or(x != z, slot != x * 2 + core))
-            def _():
-                cross_arrival(grad, crossed, slot).wait_recv()
-
-        def left(e):
-            @pl.when(jnp.logical_or(x != z, e != enc))
-            def _():
-                cross_copy(grad, crossed, e).wait_send()
-
-        def arrived():
-            each(1, N_ENC, lambda k: third_copy(grad, straight, k).wait_recv())
-            each(0, N_ENC, wait)
-
-        def sent():
-            each(1, N_ENC, lambda k: third_copy(grad, straight, k).wait_send())
-            each(0, N_ENC, left)
-
-        arrivals["third", grad] = arrived
-        sends.append(sent)
-
-    def last_phase(grad, total, shift, straight, crossed):
+            s2[grad, :, columns] = crossing[grad, :, columns]
+
+        if_other(lambda: cross_copy(grad, part).start())
+        arrivals["cross", grad] = lambda: if_other(lambda: cross_copy(grad, part).wait_recv())
+        sends.append(lambda: if_other(lambda: cross_copy(grad, part).wait_send()))
+
+    def third_phase(grad):
+        arrivals.pop(("cross", grad))()
+        x3[grad, :, :] = mm(spread, s2[grad]).astype(BF)
+        each(1, N_ENC, lambda k: third_copy(grad, k).start())
+        arrivals["third", grad] = lambda: each(
+            1, N_ENC, lambda k: third_copy(grad, k).wait_recv()
+        )
+        sends.append(lambda: each(1, N_ENC, lambda k: third_copy(grad, k).wait_send()))
+
+    def last_phase(grad, total, shift):
         arrivals.pop(("third", grad))()
-        mine = x3[grad, pl.ds(aligned(enc * 16, 16), 16), straight].astype(F32)
+        mine = x3[grad, pl.ds(aligned(enc * 16, 16), 16), :].astype(F32)
         for k in (2, 4, 6):
-            mine = mine + r3[grad, k - 1, :, straight].astype(F32)
-        theirs = r3[grad, 0, :, straight].astype(F32)
+            mine = mine + r3[grad, k - 1].astype(F32)
+        theirs = r3[grad, 0].astype(F32)
         for k in (3, 5, 7):
-            theirs = theirs + r3[grad, k - 1, :, straight].astype(F32)
-        for half, value in ((core, mine), (1 - core, theirs)):
-            lanes = pl.ds(aligned(half * shift + straight.start, 128), straight.size)
-            total[:, lanes] = value[:10, :]
-        for half in range(2):
-            value = r4[grad, half, :, crossed].astype(F32)
-            for other_x in range(1, 4):
-                value = value + r4[grad, other_x * 2 + half, :, crossed].astype(F32)
-            total[:, pl.ds(half * shift + crossed.start, crossed.size)] = value[:10, :]
+            theirs = theirs + r3[grad, k - 1].astype(F32)
+        total[:, pl.ds(aligned(core * shift, 128), HALF)] = mine[:10, :]
+        total[:, pl.ds(aligned((1 - core) * shift, 128), HALF)] = theirs[:10, :]
 
     arrivals.pop(("pair", 1))()
     arrivals.pop(("pair", 2))()
@@ -484,15 +462,6 @@
 
     exchange_second(1, emb_in, TN)
 
-    def turn_residual(i):
-        block = pl.ds(aligned(i * 128, 128), 128)
-        resT[block, :] = res[:, block].T
-
-    each(0, 10, turn_residual)
-    mean = jnp.sum(resT[...], axis=0, keepdims=True) * (1.0 / D)
-    centred = resT[...] - mean
-    inverse = lax.rsqrt(jnp.sum(centred * centred, axis=0, keepdims=True) * (1.0 / D) + 1e-6)
-
     def back_qkv(i, carry):
         rows = pl.ds(aligned(i * 256, 256), 256)
         tile = mm(wq[rows, :], gqkvT[...])
@@ -508,9 +477,6 @@
     mean_grad = mean_grad * (1.0 / D)
     mean_cross = mean_cross * (1.0 / D)
 
-    for part in OUT_PARTS[1:] + OUT_PARTS[:1]:
-        second_phase(0, part)
-
     def residual_grad(i):
         rows = pl.ds(aligned(i * 256, 256), 256)
         normed = (resT[rows, :] - mean) * inverse
@@ -521,14 +487,16 @@
 
     each(0, 5, residual_grad)
     to_pair(3, uu.at[1, :, pl.ds(0, ROWS)], uu.at[1, :, pl.ds(ROWS, ROWS)])
-    for part in OUT_PARTS:
-        third_sum(0, part)
-    third_phase(0, OUT_STRAIGHT, OUT_CROSSED)
+    for part in OUT_PARTS[1:] + OUT_PARTS[:1]:
+        second_phase(0, part)
     arrivals.pop(("pair", 0))()
     arrivals.pop(("pair", 3))()
     for part in PATCH_PARTS:
         gradient(1, part)
         first_phase(1, part)
+
+    for part in OUT_PARTS:
+        third_sum(0, part)
 
     arrivals.pop(("deliver", 1))()
     load_text.wait()
@@ -545,16 +513,17 @@
     each(0, 5, merge)
     store_merged = local(merged, merged_hbm, 9)
     store_merged.start()
-    last_phase(0, gout, HALF, OUT_STRAIGHT, OUT_CROSSED)
+    third_phase(0)
+    last_phase(0, gout, HALF)
     store_gout = local(gout, gout_hbm, 10)
     store_gout.start()
 
-    for part in PATCH_PARTS:
+    for part in PATCH_PARTS[2:] + PATCH_PARTS[:2]:
         second_phase(1, part)
-    for part in PATCH_PARTS:
+    for part in PATCH_PARTS[2:] + PATCH_PARTS[:2]:
         third_sum(1, part)
-    third_phase(1, PATCH_STRAIGHT, PATCH_CROSSED)
-    last_phase(1, gpatch, 512, PATCH_STRAIGHT, PATCH_CROSSED)
+    third_phase(1)
+    last_phase(1, gpatch, 512)
     store_gpatch = local(gpatch, gpatch_hbm, 11)
     store_gpatch.start()
 
@@ -565,15 +534,10 @@
     store_gpatch.wait()
 
 
-def finish_kernel(a, b, c, a_out, b_out, c_out, sem):
-    copies = [
-        pltpu.make_async_copy(source, target, sem.at[i])
-        for i, (source, target) in enumerate(((a, a_out), (b, b_out), (c, c_out)))
-    ]
-    for copy in copies:
-        copy.start()
-    for copy in copies:
-        copy.wait()
+def finish_kernel(a, b, c, a_out, b_out, c_out):
+    a_out[...] = a[...]
+    b_out[...] = b[...]
+    c_out[...] = c[...]
 
 
 def shards(
@@ -581,6 +545,7 @@
 ):
     smem = pl.BlockSpec(memory_space=pltpu.SMEM)
     anywhere = pl.BlockSpec(memory_space=pl.ANY)
+    vmem = pl.BlockSpec(memory_space=pltpu.VMEM)
     dma = pltpu.SemaphoreType.DMA
     merged, grad_patch, grad_out = pl.pallas_call(
         kernel,
@@ -627,9 +592,10 @@
             pltpu.VMEM((2, 3, 4, 80, HALF), BF),
             pltpu.VMEM((2, 4, 80, HALF), BF),
             pltpu.VMEM((2, 3, 80, HALF), BF),
+            pltpu.VMEM((2, 80, HALF), BF),
+            pltpu.VMEM((2, 80, HALF), BF),
             pltpu.VMEM((2, ROWS, HALF), BF),
             pltpu.VMEM((2, 7, 16, HALF), BF),
-            pltpu.VMEM((2, 8, 16, HALF), BF),
             dma((12,)),
             dma((2, 2, N_LLM)),
             dma((2, 2, N_LLM)),
@@ -641,8 +607,8 @@
             dma((2, 3, 3)),
             dma((2, 7)),
             dma((2, 7)),
-            dma((2, 8)),
-            dma((2, 8)),
+            dma((2,)),
+            dma((2,)),
         ],
         compiler_params=pltpu.CompilerParams(
             collective_id=0, has_side_effects=True, vmem_limit_bytes=56 * 1024 * 1024
@@ -658,9 +624,8 @@
             jax.ShapeDtypeStruct((10, PIN), F32),
             jax.ShapeDtypeStruct((10, D), F32),
         ),
-        in_specs=[anywhere] * 3,
-        out_specs=(anywhere, anywhere, anywhere),
-        scratch_shapes=[dma((3,))],
+        in_specs=[vmem] * 3,
+        out_specs=(vmem, vmem, vmem),
     )(merged, grad_patch, grad_out)
     return (merged, grad_patch.T, grad_out.T)
 

time: 91.1 us -> 77.3 us (0.85)
  Pallas kernels: 89.7 us -> 75.9 us
    pallas_call x1, Pallas kernels: 18.3 us -> 1.85 us  [shards(): pl.pallas_call(finish_kernel, out_shape=(jax.ShapeDtypeStruct((SEQ, D), B...]
    pallas_call x1, Pallas kernels: 71.4 us -> 74 us  [shards(): pl.pallas_call(kernel, out_shape=(jax.ShapeDtypeStruct((SEQ, D), BF), jax...]
where the time goes in v3:
time: 77.3 us; the launch traced here: 77.2 us
  Pallas kernels  75.9 us (98%)
  between operations  1.29 us (2%)
    pallas_call x1, Pallas kernels, shards(): pl.pallas_call(kernel, out_shape=(jax.ShapeDtypeStruct((SEQ, D), BF), jax...  74 us
    pallas_call x1, Pallas kernels, shards(): pl.pallas_call(finish_kernel, out_shape=(jax.ShapeDtypeStruct((SEQ, D), B...  1.85 us

profile of v3, /device:TPU:1, one launch (start us, length us, event | category | flops | bytes accessed | tf_op | source)
XLA Modules:
  0.0 77.2 jit_solution(243537463318387903)
XLA Ops:
  1.3 74.0 %shard_map.112 = (bf16[160,1280]{1,0:T(8,128)(2,1)}, f32[10,1152]{1,0:T(8,128)}, f32[10,1280]{1,0:T(8,128)}) custom-call(s32[1,128]{1,0:T(1,128)} %bitcast.3, s32[1,1]{1,0:T(1,128)S(6)} %copy.12.start_ref, s32[128,1,128]{2,1,0:T(1,128)} %seg_hbm.1, bf16[128,1152]{1,0:T(8,128)(2,1)} %patches_hbm.1, bf16[160,1280]{1,0:T(8,128)(2,1)} %text_hbm.1, ...), custom_call_target="tpu_custom_call" | custom-call | tf_op jit(solution)/shard_map/pallas_call | solution.py:550
  75.3 1.9 %shard_map.113 = (bf16[160,1280]{1,0:T(8,128)(2,1)}, f32[10,1152]{1,0:T(8,128)}, f32[10,1280]{1,0:T(8,128)}) custom-call(bf16[160,1280]{1,0:T(8,128)(2,1)} %get-tuple-element.9.a, f32[10,1152]{1,0:T(8,128)} %get-tuple-element.10.b, f32[10,1280]{1,0:T(8,128)} %get-tuple-element.11.c), custom_call_target="tpu_custom_call" | custom-call | tf_op jit(solution)/shard_map/pallas_call | solution.py:620

commit v4 on v3

--- a/solution.py
+++ b/solution.py
@@ -36,7 +36,7 @@
 
 
 def aligned(value, unit):
-    return pl.multiple_of(value, unit)
+    return value if isinstance(value, int) else pl.multiple_of(value, unit)
 
 
 def each(low, high, body):
@@ -210,11 +210,9 @@
 
     load_wp.wait()
 
-    def project(i):
-        columns = pl.ds(aligned(i * 256, 256), 256)
+    for i in range(5):
+        columns = pl.ds(256 * i, 256)
         res[:, columns] = mm(pat[...], wp[:, columns])
-
-    each(0, 5, project)
     for i in range(4):
         rows = pl.ds(32 * i, 32)
         values = res[rows, :]
@@ -222,24 +220,20 @@
         inverse = lax.rsqrt(jnp.mean(centred * centred, axis=1, keepdims=True) + 1e-6)
         nlow[rows, :] = (centred * inverse).astype(BF)
 
-    def turn_residual(i):
-        block = pl.ds(aligned(i * 128, 128), 128)
+    for i in range(10):
+        block = pl.ds(128 * i, 128)
         resT[block, :] = res[:, block].T
-
-    each(0, 10, turn_residual)
     mean = jnp.sum(resT[...], axis=0, keepdims=True) * (1.0 / D)
     centred = resT[...] - mean
     inverse = lax.rsqrt(jnp.sum(centred * centred, axis=0, keepdims=True) * (1.0 / D) + 1e-6)
 
-    def project_qkv(i):
-        columns = pl.ds(aligned(i * 256, 256), 256)
+    for i in range(15):
+        if i % 5 == 0:
+            load_wq[i // 5].wait()
+        columns = pl.ds(256 * i, 256)
         tile = mm(nlow[...], wq[:, columns]).astype(BF)
         qkv[:, columns] = tile
         qkvT[columns, :] = tile.T
-
-    for i in range(3):
-        load_wq[i].wait()
-        each(5 * i, 5 * i + 5, project_qkv)
 
     exchange_second(0, up, NN)
 
@@ -264,52 +258,40 @@
             values = qkvT[pl.ds(aligned(2 * D + base + 80 * j, 16), 80), :]
             attT[head, :] = mm(values, low).astype(BF)
 
-    each(0, 2, forward_heads)
-
-    def turn_attended(i):
-        block = pl.ds(aligned(i * 128, 128), 128)
+    for g in range(2):
+        forward_heads(g)
+
+    for i in range(10):
+        block = pl.ds(128 * i, 128)
         att[:, block] = attT[block, :].T
-
-    each(0, 10, turn_attended)
     to_pair(
         1, att.at[:, pl.ds(aligned((1 - core) * HALF, 128), HALF)], aa.at[0, pl.ds(ROWS, ROWS)]
     )
     aa[0, pl.ds(0, ROWS), :] = att[:, pl.ds(aligned(core * HALF, 128), HALF)]
 
+    load_wo.wait()
+    for i in range(5):
+        columns = pl.ds(256 * i, 256)
+        sent1[1, :, columns] = (res[:, columns] + mm(att[...], wo[:, columns])).astype(BF)
+    exchange_first(1)
+
     arrivals.pop(("deliver", 0))()
 
-    def turn_upstream(i):
-        block = pl.ds(aligned(i * 128, 128), 128)
+    for i in range(10):
+        block = pl.ds(128 * i, 128)
         upT[block, :] = up[:, block].T
-
-    each(0, 10, turn_upstream)
     to_pair(2, upT, uu.at[0, :, pl.ds(ROWS, ROWS)])
     uu[0, :, pl.ds(0, ROWS)] = upT[...]
 
-    load_wo.wait()
-
-    def project_out(i):
-        columns = pl.ds(aligned(i * 256, 256), 256)
-        sent1[1, :, columns] = (res[:, columns] + mm(att[...], wo[:, columns])).astype(BF)
-
-    each(0, 5, project_out)
-    exchange_first(1)
-
-    def project_back(i):
-        rows = pl.ds(aligned(i * 256, 256), 256)
+    for i in range(5):
+        rows = pl.ds(256 * i, 256)
         gaT[rows, :] = mm(wo[rows, :], upT[...]).astype(BF)
-
-    each(0, 5, project_back)
 
     def gradient(grad, part):
         columns, _ = part
 
-        def block(b):
-            rows = pl.ds(aligned(b * 320, 16), 320)
-            total = mm(uu[grad, rows, :], aa[grad, :, columns])
-            gt[grad, b, :, :, columns] = total.astype(BF).reshape(4, 80, columns.size)
-
-        each(0, 4, block)
+        total = mm(uu[grad], aa[grad, :, columns])
+        gt[grad, :, :, :, columns] = total.astype(BF).reshape(4, 4, 80, columns.size)
 
     def first_copy(grad, part, k):
         columns, kind = part
@@ -458,34 +440,30 @@
             gqkvT[head_k, :] = mm(qkvT[head, :], low, NT).astype(BF)
             gqkvT[head_v, :] = mm(rows, plT[block, :], NT).astype(BF)
 
-    each(0, 2, backward_heads)
+    for g in range(2):
+        backward_heads(g)
 
     exchange_second(1, emb_in, TN)
 
-    def back_qkv(i, carry):
-        rows = pl.ds(aligned(i * 256, 256), 256)
+    mean_grad = jnp.zeros((1, ROWS), F32)
+    mean_cross = jnp.zeros((1, ROWS), F32)
+    for i in range(5):
+        rows = pl.ds(256 * i, 256)
         tile = mm(wq[rows, :], gqkvT[...])
         gnT[rows, :] = tile
         normed = (resT[rows, :] - mean) * inverse
-        return (
-            carry[0] + jnp.sum(tile, axis=0, keepdims=True),
-            carry[1] + jnp.sum(tile * normed, axis=0, keepdims=True),
-        )
-
-    zero = jnp.zeros((1, ROWS), F32)
-    mean_grad, mean_cross = lax.fori_loop(0, 5, back_qkv, (zero, zero))
+        mean_grad = mean_grad + jnp.sum(tile, axis=0, keepdims=True)
+        mean_cross = mean_cross + jnp.sum(tile * normed, axis=0, keepdims=True)
     mean_grad = mean_grad * (1.0 / D)
     mean_cross = mean_cross * (1.0 / D)
 
-    def residual_grad(i):
-        rows = pl.ds(aligned(i * 256, 256), 256)
+    for i in range(5):
+        rows = pl.ds(256 * i, 256)
         normed = (resT[rows, :] - mean) * inverse
         total = upT[rows, :].astype(F32) + inverse * (
             gnT[rows, :] - mean_grad - normed * mean_cross
         )
         uu[1, rows, pl.ds(0, ROWS)] = total.astype(BF)
-
-    each(0, 5, residual_grad)
     to_pair(3, uu.at[1, :, pl.ds(0, ROWS)], uu.at[1, :, pl.ds(ROWS, ROWS)])
     for part in OUT_PARTS[1:] + OUT_PARTS[:1]:
         second_phase(0, part)
@@ -503,23 +481,21 @@
     position = iota((SEQ, ROWS), 0)
     put = (position == iota((SEQ, ROWS), 1) + start).astype(F32).astype(BF)
 
-    def merge(i):
-        columns = pl.ds(aligned(i * 256, 256), 256)
+    place = iota((SEQ, 256), 0)
+    inside = jnp.logical_and(place >= start, place < start + ROWS)
+    for i in range(5):
+        columns = pl.ds(256 * i, 256)
         placed = mm(put, emb_in[:, columns])
-        place = iota((SEQ, 256), 0)
-        inside = jnp.logical_and(place >= start, place < start + ROWS)
         merged[:, columns] = jnp.where(inside, placed, text[:, columns].astype(F32)).astype(BF)
-
-    each(0, 5, merge)
     store_merged = local(merged, merged_hbm, 9)
     store_merged.start()
     third_phase(0)
+
+    for part in PATCH_PARTS[2:] + PATCH_PARTS[:2]:
+        second_phase(1, part)
     last_phase(0, gout, HALF)
     store_gout = local(gout, gout_hbm, 10)
     store_gout.start()
-
-    for part in PATCH_PARTS[2:] + PATCH_PARTS[:2]:
-        second_phase(1, part)
     for part in PATCH_PARTS[2:] + PATCH_PARTS[:2]:
         third_sum(1, part)
     third_phase(1)

time: 77.3 us -> 72 us (0.931)
  Pallas kernels: 75.9 us -> 70.6 us
    pallas_call x1, Pallas kernels: 74 us -> 68.7 us  [shards(): pl.pallas_call(kernel, out_shape=(jax.ShapeDtypeStruct((SEQ, D), BF), jax...]
where the time goes in v4:
time: 72 us; the launch traced here: 71.8 us
  Pallas kernels  70.6 us (98%)
  between operations  1.29 us (2%)
    pallas_call x1, Pallas kernels, shards(): pl.pallas_call(kernel, out_shape=(jax.ShapeDtypeStruct((SEQ, D), BF), jax...  68.7 us
    pallas_call x1, Pallas kernels, shards(): pl.pallas_call(finish_kernel, out_shape=(jax.ShapeDtypeStruct((SEQ, D), B...  1.85 us

profile of v4, /device:TPU:1, one launch (start us, length us, event | category | flops | bytes accessed | tf_op | source)
XLA Modules:
  0.0 71.8 jit_solution(13423643651909746730)
XLA Ops:
  1.3 68.7 %shard_map.112 = (bf16[160,1280]{1,0:T(8,128)(2,1)}, f32[10,1152]{1,0:T(8,128)}, f32[10,1280]{1,0:T(8,128)}) custom-call(s32[1,128]{1,0:T(1,128)} %bitcast.3, s32[1,1]{1,0:T(1,128)S(6)} %copy.12.start_ref, s32[128,1,128]{2,1,0:T(1,128)} %seg_hbm.1, bf16[128,1152]{1,0:T(8,128)(2,1)} %patches_hbm.1, bf16[160,1280]{1,0:T(8,128)(2,1)} %text_hbm.1, ...), custom_call_target="tpu_custom_call" | custom-call | tf_op jit(solution)/shard_map/pallas_call | solution.py:526
  70.0 1.9 %shard_map.113 = (bf16[160,1280]{1,0:T(8,128)(2,1)}, f32[10,1152]{1,0:T(8,128)}, f32[10,1280]{1,0:T(8,128)}) custom-call(bf16[160,1280]{1,0:T(8,128)(2,1)} %get-tuple-element.9.a, f32[10,1152]{1,0:T(8,128)} %get-tuple-element.10.b, f32[10,1280]{1,0:T(8,128)} %get-tuple-element.11.c), custom_call_target="tpu_custom_call" | custom-call | tf_op jit(solution)/shard_map/pallas_call | solution.py:596

commit v5 on v4

--- a/solution.py
+++ b/solution.py
@@ -40,11 +40,8 @@
 
 
 def each(low, high, body):
-    def step(i, carry):
+    for i in range(low, high):
         body(i)
-        return carry
-
-    lax.fori_loop(low, high, step, 0)
 
 
 def head_window(j):
@@ -465,7 +462,7 @@
         )
         uu[1, rows, pl.ds(0, ROWS)] = total.astype(BF)
     to_pair(3, uu.at[1, :, pl.ds(0, ROWS)], uu.at[1, :, pl.ds(ROWS, ROWS)])
-    for part in OUT_PARTS[1:] + OUT_PARTS[:1]:
+    for part in OUT_PARTS[1:]:
         second_phase(0, part)
     arrivals.pop(("pair", 0))()
     arrivals.pop(("pair", 3))()
@@ -473,7 +470,7 @@
         gradient(1, part)
         first_phase(1, part)
 
-    for part in OUT_PARTS:
+    for part in OUT_PARTS[1:]:
         third_sum(0, part)
 
     arrivals.pop(("deliver", 1))()
@@ -489,16 +486,18 @@
         merged[:, columns] = jnp.where(inside, placed, text[:, columns].astype(F32)).astype(BF)
     store_merged = local(merged, merged_hbm, 9)
     store_merged.start()
-    third_phase(0)
+    second_phase(0, OUT_PARTS[0])
 
     for part in PATCH_PARTS[2:] + PATCH_PARTS[:2]:
         second_phase(1, part)
+    third_sum(0, OUT_PARTS[0])
+    for part in PATCH_PARTS[2:] + PATCH_PARTS[:2]:
+        third_sum(1, part)
+    third_phase(0)
+    third_phase(1)
     last_phase(0, gout, HALF)
     store_gout = local(gout, gout_hbm, 10)
     store_gout.start()
-    for part in PATCH_PARTS[2:] + PATCH_PARTS[:2]:
-        third_sum(1, part)
-    third_phase(1)
     last_phase(1, gpatch, 512)
     store_gpatch = local(gpatch, gpatch_hbm, 11)
     store_gpatch.start()

time: 72 us -> 64.9 us (0.901)
  Pallas kernels: 70.6 us -> 63.4 us
    pallas_call x1, Pallas kernels: 68.7 us -> 61.6 us  [shards(): pl.pallas_call(kernel, out_shape=(jax.ShapeDtypeStruct((SEQ, D), BF), jax...]
where the time goes in v5:
time: 64.9 us; the launch traced here: 64.7 us
  Pallas kernels  63.4 us (98%)
  between operations  1.29 us (2%)
    pallas_call x1, Pallas kernels, shards(): pl.pallas_call(kernel, out_shape=(jax.ShapeDtypeStruct((SEQ, D), BF), jax...  61.6 us
    pallas_call x1, Pallas kernels, shards(): pl.pallas_call(finish_kernel, out_shape=(jax.ShapeDtypeStruct((SEQ, D), B...  1.85 us

profile of v5, /device:TPU:1, one launch (start us, length us, event | category | flops | bytes accessed | tf_op | source)
XLA Modules:
  0.0 64.7 jit_solution(8930438021082354542)
XLA Ops:
  1.3 61.6 %shard_map.112 = (bf16[160,1280]{1,0:T(8,128)(2,1)}, f32[10,1152]{1,0:T(8,128)}, f32[10,1280]{1,0:T(8,128)}) custom-call(s32[1,128]{1,0:T(1,128)} %bitcast.3, s32[1,1]{1,0:T(1,128)S(6)} %copy.12.start_ref, s32[128,1,128]{2,1,0:T(1,128)} %seg_hbm.1, bf16[128,1152]{1,0:T(8,128)(2,1)} %patches_hbm.1, bf16[160,1280]{1,0:T(8,128)(2,1)} %text_hbm.1, ...), custom_call_target="tpu_custom_call" | custom-call | tf_op jit(solution)/shard_map/pallas_call | solution.py:525
  62.9 1.9 %shard_map.113 = (bf16[160,1280]{1,0:T(8,128)(2,1)}, f32[10,1152]{1,0:T(8,128)}, f32[10,1280]{1,0:T(8,128)}) custom-call(bf16[160,1280]{1,0:T(8,128)(2,1)} %get-tuple-element.9.a, f32[10,1152]{1,0:T(8,128)} %get-tuple-element.10.b, f32[10,1280]{1,0:T(8,128)} %get-tuple-element.11.c), custom_call_target="tpu_custom_call" | custom-call | tf_op jit(solution)/shard_map/pallas_call | solution.py:595

commit v6 on v5

--- a/solution.py
+++ b/solution.py
@@ -16,8 +16,16 @@
 HALF = 640
 SCALE = HEAD_DIM ** (-0.5)
 
-OUT_PARTS = ((pl.ds(256, 384), 2), (pl.ds(0, 128), 0), (pl.ds(128, 128), 1))
-PATCH_PARTS = ((pl.ds(0, 256), 0), (pl.ds(256, 256), 1), (pl.ds(512, 128), 2))
+OUT_PARTS = (
+    ((pl.ds(384, 256), 2), (pl.ds(0, 256), 0), (pl.ds(256, 128), 1)),
+    ((pl.ds(384, 256), 2), (pl.ds(0, 128), 0), (pl.ds(128, 256), 1)),
+)
+PATCH_PARTS = (
+    ((pl.ds(384, 128), 2), (pl.ds(0, 256), 0), (pl.ds(256, 128), 1)),
+    ((pl.ds(384, 256), 2), (pl.ds(0, 128), 0), (pl.ds(128, 256), 1)),
+)
+PARTS = (OUT_PARTS, PATCH_PARTS)
+DOT_LANES = (pl.ds(384, 256), pl.ds(0, 256), pl.ds(256, 128))
 
 BF = jnp.bfloat16
 F32 = jnp.float32
@@ -61,9 +69,9 @@
 
 
 def kernel(
-    owner_ref, start_ref, seg_hbm, patches_hbm, text_hbm, mgrad_hbm, wp_hbm, wq_hbm, wo_hbm,
+    owner_hbm, start_hbm, seg_hbm, patches_hbm, text_hbm, mgrad_hbm, wp_hbm, wq_hbm, wo_hbm,
     merged_hbm, gpatch_hbm, gout_hbm,
-    seg, pat, text, mgrad, wp, wq, wo,
+    owner, first_row, seg, pat, text, mgrad, wp, wq, wo,
     perm, sent1, recv1, sent2, emb_in, up, res, nlow, resT, qkv, qkvT, pT, plT, attT, att,
     upT, gaT, gqkvT, gnT, merged, gpatch, gout, uu, aa, gt, r1, s1, r2, crossing, s2, x3, r3,
     local_sem, ex_send, ex_recv, pair_send, pair_recv, p1_send, p1_recv, p2_send, p2_recv,
@@ -74,7 +82,6 @@
     y, x = llm // 4, llm % 4
     z, core = enc // 2, enc % 2
     device = llm * N_ENC + enc
-    start = start_ref[0, 0]
     arrivals, sends = {}, []
 
     def local(source, target, slot):
@@ -86,6 +93,8 @@
             device_id=(to_llm, to_enc), device_id_type=MESH,
         )
 
+    load_owner = local(owner_hbm, owner, 12)
+    load_start = local(start_hbm, first_row, 13)
     load_mgrad = local(mgrad_hbm, mgrad, 0)
     load_pat = local(patches_hbm, pat, 1)
     load_seg = local(seg_hbm.at[device], seg, 2)
@@ -95,7 +104,7 @@
     ]
     load_wo = local(wo_hbm, wo, 7)
     load_text = local(text_hbm, text, 8)
-    for load in (load_mgrad, load_pat, load_seg, load_wp, *load_wq, load_wo, load_text):
+    for load in (load_owner, load_start, load_mgrad, load_pat, load_seg, load_wp, *load_wq, load_wo, load_text):
         load.start()
 
     barrier = pltpu.get_barrier_semaphore()
@@ -119,11 +128,14 @@
             barrier, inc=1, device_id=(y * 4 + z, x * 2 + core), device_id_type=MESH
         )
 
+    load_owner.wait()
+    load_start.wait()
+    start = first_row[0, 0]
     lane = iota((16, 256), 1)
     row = iota((16, 256), 0)
 
     def owner_rows(s):
-        rank = owner_ref[0, s * N_ENC + enc]
+        rank = owner[0, s * N_ENC + enc]
         hit = (lane == rank * 16 + row).astype(F32)
         perm[pl.ds(aligned(s * 16, 16), 16), :] = hit.astype(BF)
 
@@ -190,7 +202,6 @@
         )
 
     exchange_first(0)
-
     other = enc + 1 - 2 * core
 
     def to_pair(slot, source, target):
@@ -270,7 +281,6 @@
     for i in range(5):
         columns = pl.ds(256 * i, 256)
         sent1[1, :, columns] = (res[:, columns] + mm(att[...], wo[:, columns])).astype(BF)
-    exchange_first(1)
 
     arrivals.pop(("deliver", 0))()
 
@@ -278,15 +288,19 @@
         block = pl.ds(128 * i, 128)
         upT[block, :] = up[:, block].T
     to_pair(2, upT, uu.at[0, :, pl.ds(ROWS, ROWS)])
+    exchange_first(1)
     uu[0, :, pl.ds(0, ROWS)] = upT[...]
 
     for i in range(5):
         rows = pl.ds(256 * i, 256)
         gaT[rows, :] = mm(wo[rows, :], upT[...]).astype(BF)
 
-    def gradient(grad, part):
-        columns, _ = part
-
+    def by_core(run):
+        for c in range(2):
+            pl.when(core == c)(lambda c=c: run(c))
+
+    def gradient(grad, index):
+        columns = DOT_LANES[index]
         total = mm(uu[grad], aa[grad, :, columns])
         gt[grad, :, :, :, columns] = total.astype(BF).reshape(4, 4, 80, columns.size)
 
@@ -333,36 +347,37 @@
             p3_send.at[grad, k - 1], p3_recv.at[grad, k - 1], llm, to,
         )
 
-    def first_phase(grad, part):
-        _, kind = part
-        for k in range(1, 4):
-            first_copy(grad, part, k).start()
-        arrivals["first", grad, kind] = lambda: [
-            first_copy(grad, part, k).wait_recv() for k in range(1, 4)
-        ]
-        sends.append(lambda: [first_copy(grad, part, k).wait_send() for k in range(1, 4)])
-
-    def second_phase(grad, part):
-        columns, kind = part
-        arrivals.pop(("first", grad, kind))()
-
-        def add(i):
-            if kind == 0:
-                own = gt[grad, y, i, :, columns]
-            else:
-                own = gt[grad, i, x if kind == 1 else z, :, columns]
-            total = own.astype(F32)
-            for k in range(3):
-                total = total + r1[grad, k, i, :, columns].astype(F32)
-            s1[grad, i, :, columns] = total.astype(BF)
-
-        each(0, 4, add)
-        for k in range(1, 4):
-            second_copy(grad, part, k).start()
-        arrivals["second", grad, kind] = lambda: [
-            second_copy(grad, part, k).wait_recv() for k in range(1, 4)
-        ]
-        sends.append(lambda: [second_copy(grad, part, k).wait_send() for k in range(1, 4)])
+    def three(grad, index, copy, act):
+        def run(c):
+            for k in range(1, 4):
+                getattr(copy(grad, PARTS[grad][c][index], k), act)()
+
+        by_core(run)
+
+    def first_phase(grad, index):
+        three(grad, index, first_copy, "start")
+        arrivals["first", grad, index] = lambda: three(grad, index, first_copy, "wait_recv")
+        sends.append(lambda: three(grad, index, first_copy, "wait_send"))
+
+    def second_phase(grad, index):
+        arrivals.pop(("first", grad, index))()
+
+        def run(c):
+            columns, kind = PARTS[grad][c][index]
+            for i in range(4):
+                if kind == 0:
+                    own = gt[grad, y, i, :, columns]
+                else:
+                    own = gt[grad, i, x if kind == 1 else z, :, columns]
+                total = own.astype(F32)
+                for k in range(3):
+                    total = total + r1[grad, k, i, :, columns].astype(F32)
+                s1[grad, i, :, columns] = total.astype(BF)
+
+        by_core(run)
+        three(grad, index, second_copy, "start")
+        arrivals["second", grad, index] = lambda: three(grad, index, second_copy, "wait_recv")
+        sends.append(lambda: three(grad, index, second_copy, "wait_send"))
 
     spread_row = iota((ROWS, 80), 0)
     spread = jnp.logical_and(
@@ -370,28 +385,35 @@
     )
     spread = spread.astype(F32).astype(BF)
 
-    def third_sum(grad, part):
-        columns, kind = part
-        arrivals.pop(("second", grad, kind))()
-        total = s1[grad, x if kind == 0 else y, :, columns].astype(F32)
-        for k in range(3):
-            total = total + r2[grad, k, :, columns].astype(F32)
-        if kind < 2:
-            s2[grad, :, columns] = total.astype(BF)
-            return
-
-        crossing[grad, :, columns] = total.astype(BF)
-
-        def if_other(run):
-            pl.when(x != z)(run)
-
-        @pl.when(x == z)
-        def _():
-            s2[grad, :, columns] = crossing[grad, :, columns]
-
-        if_other(lambda: cross_copy(grad, part).start())
-        arrivals["cross", grad] = lambda: if_other(lambda: cross_copy(grad, part).wait_recv())
-        sends.append(lambda: if_other(lambda: cross_copy(grad, part).wait_send()))
+    def cross(grad, act):
+        def run(c):
+            getattr(cross_copy(grad, PARTS[grad][c][0]), act)()
+
+        pl.when(x != z)(lambda: by_core(run))
+
+    def third_sum(grad, index):
+        arrivals.pop(("second", grad, index))()
+
+        def run(c):
+            columns, kind = PARTS[grad][c][index]
+            total = s1[grad, x if kind == 0 else y, :, columns].astype(F32)
+            for k in range(3):
+                total = total + r2[grad, k, :, columns].astype(F32)
+            if kind < 2:
+                s2[grad, :, columns] = total.astype(BF)
+                return
+
+            crossing[grad, :, columns] = total.astype(BF)
+
+            @pl.when(x == z)
+            def _():
+                s2[grad, :, columns] = crossing[grad, :, columns]
+
+        by_core(run)
+        if index == 0:
+            cross(grad, "start")
+            arrivals["cross", grad] = lambda: cross(grad, "wait_recv")
+            sends.append(lambda: cross(grad, "wait_send"))
 
     def third_phase(grad):
         arrivals.pop(("cross", grad))()
@@ -410,14 +432,22 @@
         theirs = r3[grad, 0].astype(F32)
         for k in (3, 5, 7):
             theirs = theirs + r3[grad, k - 1].astype(F32)
-        total[:, pl.ds(aligned(core * shift, 128), HALF)] = mine[:10, :]
-        total[:, pl.ds(aligned((1 - core) * shift, 128), HALF)] = theirs[:10, :]
+
+        def put_halves(c):
+            total[:, pl.ds(0, HALF)] = (mine if c == 0 else theirs)[:10, :]
+            total[:, pl.ds(shift, HALF)] = (theirs if c == 0 else mine)[:10, :]
+
+        by_core(put_halves)
+
+    @pl.when(core == 0)
+    def _():
+        s2[1, :, pl.ds(512, 128)] = jnp.zeros((80, 128), BF)
 
     arrivals.pop(("pair", 1))()
     arrivals.pop(("pair", 2))()
-    for part in OUT_PARTS:
-        gradient(0, part)
-        first_phase(0, part)
+    for index in range(3):
+        gradient(0, index)
+        first_phase(0, index)
 
     def backward_heads(g):
         base = g * HALF
@@ -440,7 +470,6 @@
     for g in range(2):
         backward_heads(g)
 
-    exchange_second(1, emb_in, TN)
 
     mean_grad = jnp.zeros((1, ROWS), F32)
     mean_cross = jnp.zeros((1, ROWS), F32)
@@ -451,6 +480,7 @@
         normed = (resT[rows, :] - mean) * inverse
         mean_grad = mean_grad + jnp.sum(tile, axis=0, keepdims=True)
         mean_cross = mean_cross + jnp.sum(tile * normed, axis=0, keepdims=True)
+    exchange_second(1, emb_in, TN)
     mean_grad = mean_grad * (1.0 / D)
     mean_cross = mean_cross * (1.0 / D)
 
@@ -462,16 +492,16 @@
         )
         uu[1, rows, pl.ds(0, ROWS)] = total.astype(BF)
     to_pair(3, uu.at[1, :, pl.ds(0, ROWS)], uu.at[1, :, pl.ds(ROWS, ROWS)])
-    for part in OUT_PARTS[1:]:
-        second_phase(0, part)
+    second_phase(0, 1)
+    second_phase(0, 2)
     arrivals.pop(("pair", 0))()
     arrivals.pop(("pair", 3))()
-    for part in PATCH_PARTS:
-        gradient(1, part)
-        first_phase(1, part)
-
-    for part in OUT_PARTS[1:]:
-        third_sum(0, part)
+    for index in range(3):
+        gradient(1, index)
+        first_phase(1, index)
+
+    third_sum(0, 1)
+    third_sum(0, 2)
 
     arrivals.pop(("deliver", 1))()
     load_text.wait()
@@ -486,14 +516,15 @@
         merged[:, columns] = jnp.where(inside, placed, text[:, columns].astype(F32)).astype(BF)
     store_merged = local(merged, merged_hbm, 9)
     store_merged.start()
-    second_phase(0, OUT_PARTS[0])
-
-    for part in PATCH_PARTS[2:] + PATCH_PARTS[:2]:
-        second_phase(1, part)
-    third_sum(0, OUT_PARTS[0])
-    for part in PATCH_PARTS[2:] + PATCH_PARTS[:2]:
-        third_sum(1, part)
+    second_phase(0, 0)
+    second_phase(1, 0)
+    second_phase(1, 1)
+    second_phase(1, 2)
+    third_sum(0, 0)
+    third_sum(1, 0)
     third_phase(0)
+    third_sum(1, 1)
+    third_sum(1, 2)
     third_phase(1)
     last_phase(0, gout, HALF)
     store_gout = local(gout, gout_hbm, 10)
@@ -518,7 +549,6 @@
 def shards(
     patches, image_seg, owner_slot, place_start, text_embeds, merged_grad, w_patch, w_qkv, w_out
 ):
-    smem = pl.BlockSpec(memory_space=pltpu.SMEM)
     anywhere = pl.BlockSpec(memory_space=pl.ANY)
     vmem = pl.BlockSpec(memory_space=pltpu.VMEM)
     dma = pltpu.SemaphoreType.DMA
@@ -529,9 +559,11 @@
             jax.ShapeDtypeStruct((10, PIN), F32),
             jax.ShapeDtypeStruct((10, D), F32),
         ),
-        in_specs=[smem, smem] + [anywhere] * 7,
+        in_specs=[anywhere] * 9,
         out_specs=(anywhere, anywhere, anywhere),
         scratch_shapes=[
+            pltpu.SMEM((1, ROWS), jnp.int32),
+            pltpu.SMEM((1, 1), jnp.int32),
             pltpu.VMEM((1, ROWS), jnp.int32),
             pltpu.VMEM((ROWS, PIN), BF),
             pltpu.VMEM((SEQ, D), BF),
@@ -571,7 +603,7 @@
             pltpu.VMEM((2, 80, HALF), BF),
             pltpu.VMEM((2, ROWS, HALF), BF),
             pltpu.VMEM((2, 7, 16, HALF), BF),
-            dma((12,)),
+            dma((14,)),
             dma((2, 2, N_LLM)),
             dma((2, 2, N_LLM)),
             dma((4,)),

time: 64.9 us -> 63.3 us (0.975)
  Pallas kernels: 63.4 us -> 61.9 us
    pallas_call x1, Pallas kernels: 61.6 us -> 60.1 us  [shards(): pl.pallas_call(kernel, out_shape=(jax.ShapeDtypeStruct((SEQ, D), BF), jax...]
where the time goes in v6:
time: 63.3 us; the launch traced here: 63.2 us
  Pallas kernels  61.9 us (98%)
  between operations  1.29 us (2%)
    pallas_call x1, Pallas kernels, shards(): pl.pallas_call(kernel, out_shape=(jax.ShapeDtypeStruct((SEQ, D), BF), jax...  60.1 us
    pallas_call x1, Pallas kernels, shards(): pl.pallas_call(finish_kernel, out_shape=(jax.ShapeDtypeStruct((SEQ, D), B...  1.85 us

profile of v6, /device:TPU:1, one launch (start us, length us, event | category | flops | bytes accessed | tf_op | source)
XLA Modules:
  0.0 63.2 jit_solution(4955458100923392745)
XLA Ops:
  1.3 60.1 %shard_map.112 = (bf16[160,1280]{1,0:T(8,128)(2,1)}, f32[10,1152]{1,0:T(8,128)}, f32[10,1280]{1,0:T(8,128)}) custom-call(s32[1,128]{1,0:T(1,128)} %bitcast.3, s32[1,1]{1,0:T(1,128)S(6)} %copy.12.start_hbm, s32[128,1,128]{2,1,0:T(1,128)} %seg_hbm.1, bf16[128,1152]{1,0:T(8,128)(2,1)} %patches_hbm.1, bf16[160,1280]{1,0:T(8,128)(2,1)} %text_hbm.1, ...), custom_call_target="tpu_custom_call" | custom-call | tf_op jit(solution)/shard_map/pallas_call | solution.py:555
  61.3 1.9 %shard_map.113 = (bf16[160,1280]{1,0:T(8,128)(2,1)}, f32[10,1152]{1,0:T(8,128)}, f32[10,1280]{1,0:T(8,128)}) custom-call(bf16[160,1280]{1,0:T(8,128)(2,1)} %get-tuple-element.9.a, f32[10,1152]{1,0:T(8,128)} %get-tuple-element.10.b, f32[10,1280]{1,0:T(8,128)} %get-tuple-element.11.c), custom_call_target="tpu_custom_call" | custom-call | tf_op jit(solution)/shard_map/pallas_call | solution.py:627

commit v7 on v6

--- a/solution.py
+++ b/solution.py
@@ -18,11 +18,11 @@
 
 OUT_PARTS = (
     ((pl.ds(384, 256), 2), (pl.ds(0, 256), 0), (pl.ds(256, 128), 1)),
-    ((pl.ds(384, 256), 2), (pl.ds(0, 128), 0), (pl.ds(128, 256), 1)),
+    ((pl.ds(384, 256), 3), (pl.ds(0, 128), 0), (pl.ds(128, 256), 1)),
 )
 PATCH_PARTS = (
     ((pl.ds(384, 128), 2), (pl.ds(0, 256), 0), (pl.ds(256, 128), 1)),
-    ((pl.ds(384, 256), 2), (pl.ds(0, 128), 0), (pl.ds(128, 256), 1)),
+    ((pl.ds(384, 256), 3), (pl.ds(0, 128), 0), (pl.ds(128, 256), 1)),
 )
 PARTS = (OUT_PARTS, PATCH_PARTS)
 DOT_LANES = (pl.ds(384, 256), pl.ds(0, 256), pl.ds(256, 128))
@@ -72,7 +72,7 @@
     owner_hbm, start_hbm, seg_hbm, patches_hbm, text_hbm, mgrad_hbm, wp_hbm, wq_hbm, wo_hbm,
     merged_hbm, gpatch_hbm, gout_hbm,
     owner, first_row, seg, pat, text, mgrad, wp, wq, wo,
-    perm, sent1, recv1, sent2, emb_in, up, res, nlow, resT, qkv, qkvT, pT, plT, attT, att,
+    perm, sent1, recv1, sent2, emb_in, up, res, nlow, resT, qkv, qkvT, pT, probs, attT, att,
     upT, gaT, gqkvT, gnT, merged, gpatch, gout, uu, aa, gt, r1, s1, r2, crossing, s2, x3, r3,
     local_sem, ex_send, ex_recv, pair_send, pair_recv, p1_send, p1_recv, p2_send, p2_recv,
     p3_send, p3_recv, p4_send, p4_recv,
@@ -122,10 +122,13 @@
     each(1, N_LLM, greet_llm)
     each(1, N_ENC, greet_enc)
 
-    @pl.when(x != z)
+    turned = jnp.where(core == 0, x, y)
+    mate_llm, mate_enc = jnp.where(core == 0, y * 4 + z, z * 4 + x), turned * 2 + core
+
+    @pl.when(turned != z)
     def _():
         pl.semaphore_signal(
-            barrier, inc=1, device_id=(y * 4 + z, x * 2 + core), device_id_type=MESH
+            barrier, inc=1, device_id=(mate_llm, mate_enc), device_id_type=MESH
         )
 
     load_owner.wait()
@@ -145,7 +148,7 @@
     take = (iota((ROWS, SEQ), 1) == iota((ROWS, SEQ), 0) + start).astype(F32).astype(BF)
     sent1[0, :, :] = mm(take, mgrad[...]).astype(BF)
 
-    pl.semaphore_wait(barrier, N_LLM - 1 + N_ENC - 1 + (x != z).astype(jnp.int32))
+    pl.semaphore_wait(barrier, N_LLM - 1 + N_ENC - 1 + (turned != z).astype(jnp.int32))
 
     def piece(ref, j):
         return ref.at[pl.ds(aligned(j // 2 * 16, 16), 16), pl.ds(aligned(j % 2 * HALF, 128), HALF)]
@@ -262,7 +265,7 @@
             probability = weights / jnp.sum(weights, axis=0, keepdims=True)
             low = probability.astype(BF)
             pT[block, :] = probability
-            plT[block, :] = low
+            probs[block, :] = low.T
             values = qkvT[pl.ds(aligned(2 * D + base + 80 * j, 16), 80), :]
             attT[head, :] = mm(values, low).astype(BF)
 
@@ -314,15 +317,16 @@
             source, to_llm, to_enc = gt.at[grad, :, to, :, columns], y * 4 + to, enc
         else:
             to = (z + k) % 4
-            source, to_llm, to_enc = gt.at[grad, :, to, :, columns], llm, to * 2 + core
+            source = gt.at[grad, :, to, :, columns] if kind == 2 else gt.at[grad, to, :, :, columns]
+            to_llm, to_enc = llm, to * 2 + core
         return remote(
             source, r1.at[grad, k - 1, :, :, columns],
-            p1_send.at[grad, kind, k - 1], p1_recv.at[grad, kind, k - 1], to_llm, to_enc,
+            p1_send.at[grad, min(kind, 2), k - 1], p1_recv.at[grad, min(kind, 2), k - 1], to_llm, to_enc,
         )
 
     def second_copy(grad, part, k):
         columns, kind = part
-        if kind == 0:
+        if kind in (0, 3):
             to = (x + k) % 4
             to_llm = y * 4 + to
         else:
@@ -330,14 +334,14 @@
             to_llm = to * 4 + x
         return remote(
             s1.at[grad, to, :, columns], r2.at[grad, k - 1, :, columns],
-            p2_send.at[grad, kind, k - 1], p2_recv.at[grad, kind, k - 1], to_llm, enc,
+            p2_send.at[grad, min(kind, 2), k - 1], p2_recv.at[grad, min(kind, 2), k - 1], to_llm, enc,
         )
 
     def cross_copy(grad, part):
         columns, _ = part
         return remote(
             crossing.at[grad, :, columns], s2.at[grad, :, columns],
-            p4_send.at[grad], p4_recv.at[grad], y * 4 + z, x * 2 + core,
+            p4_send.at[grad], p4_recv.at[grad], mate_llm, mate_enc,
         )
 
     def third_copy(grad, k):
@@ -365,8 +369,8 @@
         def run(c):
             columns, kind = PARTS[grad][c][index]
             for i in range(4):
-                if kind == 0:
-                    own = gt[grad, y, i, :, columns]
+                if kind in (0, 3):
+                    own = gt[grad, z if kind else y, i, :, columns]
                 else:
                     own = gt[grad, i, x if kind == 1 else z, :, columns]
                 total = own.astype(F32)
@@ -389,14 +393,14 @@
         def run(c):
             getattr(cross_copy(grad, PARTS[grad][c][0]), act)()
 
-        pl.when(x != z)(lambda: by_core(run))
+        pl.when(turned != z)(lambda: by_core(run))
 
     def third_sum(grad, index):
         arrivals.pop(("second", grad, index))()
 
         def run(c):
             columns, kind = PARTS[grad][c][index]
-            total = s1[grad, x if kind == 0 else y, :, columns].astype(F32)
+            total = s1[grad, x if kind in (0, 3) else y, :, columns].astype(F32)
             for k in range(3):
                 total = total + r2[grad, k, :, columns].astype(F32)
             if kind < 2:
@@ -405,7 +409,7 @@
 
             crossing[grad, :, columns] = total.astype(BF)
 
-            @pl.when(x == z)
+            @pl.when(turned == z)
             def _():
                 s2[grad, :, columns] = crossing[grad, :, columns]
 
@@ -465,7 +469,7 @@
             low = (probability * (grad_prob - weighted) * SCALE).astype(BF)
             gqkvT[head, :] = mm(qkvT[head_k, :], low).astype(BF)
             gqkvT[head_k, :] = mm(qkvT[head, :], low, NT).astype(BF)
-            gqkvT[head_v, :] = mm(rows, plT[block, :], NT).astype(BF)
+            gqkvT[head_v, :] = mm(rows, probs[block, :]).astype(BF)
 
     for g in range(2):
         backward_heads(g)

time: 63.3 us -> 62.1 us (0.981)
  Pallas kernels: 61.9 us -> 60.6 us
    pallas_call x1, Pallas kernels: 60.1 us -> 58.8 us  [shards(): pl.pallas_call(kernel, out_shape=(jax.ShapeDtypeStruct((SEQ, D), BF), jax...]
where the time goes in v7:
time: 62.1 us; the launch traced here: 61.9 us
  Pallas kernels  60.6 us (98%)
  between operations  1.29 us (2%)
    pallas_call x1, Pallas kernels, shards(): pl.pallas_call(kernel, out_shape=(jax.ShapeDtypeStruct((SEQ, D), BF), jax...  58.8 us
    pallas_call x1, Pallas kernels, shards(): pl.pallas_call(finish_kernel, out_shape=(jax.ShapeDtypeStruct((SEQ, D), B...  1.85 us

profile of v7, /device:TPU:1, one launch (start us, length us, event | category | flops | bytes accessed | tf_op | source)
XLA Modules:
  0.0 61.9 jit_solution(1297161510344704358)
XLA Ops:
  1.3 58.8 %shard_map.112 = (bf16[160,1280]{1,0:T(8,128)(2,1)}, f32[10,1152]{1,0:T(8,128)}, f32[10,1280]{1,0:T(8,128)}) custom-call(s32[1,128]{1,0:T(1,128)} %bitcast.3, s32[1,1]{1,0:T(1,128)S(6)} %copy.12.start_hbm, s32[128,1,128]{2,1,0:T(1,128)} %seg_hbm.1, bf16[128,1152]{1,0:T(8,128)(2,1)} %patches_hbm.1, bf16[160,1280]{1,0:T(8,128)(2,1)} %text_hbm.1, ...), custom_call_target="tpu_custom_call" | custom-call | tf_op jit(solution)/shard_map/pallas_call | solution.py:559
  60.1 1.9 %shard_map.113 = (bf16[160,1280]{1,0:T(8,128)(2,1)}, f32[10,1152]{1,0:T(8,128)}, f32[10,1280]{1,0:T(8,128)}) custom-call(bf16[160,1280]{1,0:T(8,128)(2,1)} %get-tuple-element.9.a, f32[10,1152]{1,0:T(8,128)} %get-tuple-element.10.b, f32[10,1280]{1,0:T(8,128)} %get-tuple-element.11.c), custom_call_target="tpu_custom_call" | custom-call | tf_op jit(solution)/shard_map/pallas_call | solution.py:631

commit v8 on v7

--- a/solution.py
+++ b/solution.py
@@ -25,6 +25,7 @@
     ((pl.ds(384, 256), 3), (pl.ds(0, 128), 0), (pl.ds(128, 256), 1)),
 )
 PARTS = (OUT_PARTS, PATCH_PARTS)
+PEERS = (10, 6, 9, 11, 14, 2, 5, 7, 8, 13, 15, 1, 3, 4, 12)
 DOT_LANES = (pl.ds(384, 256), pl.ds(0, 256), pl.ds(256, 128))
 
 BF = jnp.bfloat16
@@ -50,6 +51,11 @@
 def each(low, high, body):
     for i in range(low, high):
         body(i)
+
+
+def each_peer(body):
+    for k in PEERS:
+        body(k)
 
 
 def head_window(j):
@@ -153,53 +159,59 @@
     def piece(ref, j):
         return ref.at[pl.ds(aligned(j // 2 * 16, 16), 16), pl.ds(aligned(j % 2 * HALF, 128), HALF)]
 
+    def ahead(k):
+        return (y + k // 4) % 4 * 4 + (x + k % 4) % 4
+
+    def behind(k):
+        return (y + 4 - k // 4) % 4 * 4 + (x + 4 - k % 4) % 4
+
     def scatter(way, k):
-        to = (llm + k) % N_LLM
+        to = ahead(k)
         return remote(
             piece(sent1.at[way], to), recv1.at[way, pl.ds(aligned(llm * 16, 16), 16)],
             ex_send.at[way, 0, k], ex_recv.at[way, 0, k], to, enc,
         )
 
     def scatter_arrival(way, k):
-        source = (llm + N_LLM - k) % N_LLM
+        source = behind(k)
         return remote(
             piece(sent1.at[way], llm), recv1.at[way, pl.ds(aligned(source * 16, 16), 16)],
-            ex_send.at[way, 0, k], ex_recv.at[way, 0, k], (llm + k) % N_LLM, enc,
+            ex_send.at[way, 0, k], ex_recv.at[way, 0, k], ahead(k), enc,
         )
 
     def deliver(way, target, k):
-        to = (llm + k) % N_LLM
+        to = ahead(k)
         return remote(
             sent2.at[way, pl.ds(aligned(to * 16, 16), 16)], piece(target, llm),
             ex_send.at[way, 1, k], ex_recv.at[way, 1, k], to, enc,
         )
 
     def deliver_arrival(way, target, k):
-        source = (llm + N_LLM - k) % N_LLM
+        source = behind(k)
         return remote(
             sent2.at[way, pl.ds(aligned(llm * 16, 16), 16)], piece(target, source),
-            ex_send.at[way, 1, k], ex_recv.at[way, 1, k], (llm + k) % N_LLM, enc,
+            ex_send.at[way, 1, k], ex_recv.at[way, 1, k], ahead(k), enc,
         )
 
     def own_piece(ref):
         return ref[pl.ds(aligned(llm // 2 * 16, 16), 16), pl.ds(aligned(llm % 2 * HALF, 128), HALF)]
 
     def exchange_first(way):
-        each(1, N_LLM, lambda k: scatter(way, k).start())
-        arrivals["scatter", way] = lambda: each(
-            1, N_LLM, lambda k: scatter_arrival(way, k).wait_recv()
-        )
-        sends.append(lambda: each(1, N_LLM, lambda k: scatter(way, k).wait_send()))
+        each_peer(lambda k: scatter(way, k).start())
+        arrivals["scatter", way] = lambda: each_peer(
+            lambda k: scatter_arrival(way, k).wait_recv()
+        )
+        sends.append(lambda: each_peer(lambda k: scatter(way, k).wait_send()))
         recv1[way, pl.ds(aligned(llm * 16, 16), 16), :] = own_piece(sent1.at[way])
 
     def exchange_second(way, target, dims):
         arrivals.pop(("scatter", way))()
         sent2[way, :, :] = mm(perm[...], recv1[way], dims).astype(BF)
-        each(1, N_LLM, lambda k: deliver(way, target, k).start())
-        arrivals["deliver", way] = lambda: each(
-            1, N_LLM, lambda k: deliver_arrival(way, target, k).wait_recv()
-        )
-        sends.append(lambda: each(1, N_LLM, lambda k: deliver(way, target, k).wait_send()))
+        each_peer(lambda k: deliver(way, target, k).start())
+        arrivals["deliver", way] = lambda: each_peer(
+            lambda k: deliver_arrival(way, target, k).wait_recv()
+        )
+        sends.append(lambda: each_peer(lambda k: deliver(way, target, k).wait_send()))
         target[pl.ds(aligned(llm // 2 * 16, 16), 16), pl.ds(aligned(llm % 2 * HALF, 128), HALF)] = (
             sent2[way, pl.ds(aligned(llm * 16, 16), 16), :]
         )
@@ -353,7 +365,7 @@
 
     def three(grad, index, copy, act):
         def run(c):
-            for k in range(1, 4):
+            for k in (2, 1, 3):
                 getattr(copy(grad, PARTS[grad][c][index], k), act)()
 
         by_core(run)
@@ -422,7 +434,7 @@
     def third_phase(grad):
         arrivals.pop(("cross", grad))()
         x3[grad, :, :] = mm(spread, s2[grad]).astype(BF)
-        each(1, N_ENC, lambda k: third_copy(grad, k).start())
+        [third_copy(grad, k).start() for k in (4, 3, 5, 2, 6, 7, 1)]
         arrivals["third", grad] = lambda: each(
             1, N_ENC, lambda k: third_copy(grad, k).wait_recv()
         )
@@ -544,17 +556,23 @@
     store_gpatch.wait()
 
 
-def finish_kernel(a, b, c, a_out, b_out, c_out):
-    a_out[...] = a[...]
-    b_out[...] = b[...]
-    c_out[...] = c[...]
+def finish_kernel(a, b, c, a_out, b_out, c_out, a_held, b_held, c_held, sem):
+    arrays = ((a, a_held, a_out), (b, b_held, b_out), (c, c_held, c_out))
+    loads = [pltpu.make_async_copy(v[0], v[1], sem.at[i]) for i, v in enumerate(arrays)]
+    stores = [pltpu.make_async_copy(v[1], v[2], sem.at[3 + i]) for i, v in enumerate(arrays)]
+    for load in loads:
+        load.start()
+    for load, store in zip(loads, stores):
+        load.wait()
+        store.start()
+    for store in stores:
+        store.wait()
 
 
 def shards(
     patches, image_seg, owner_slot, place_start, text_embeds, merged_grad, w_patch, w_qkv, w_out
 ):
     anywhere = pl.BlockSpec(memory_space=pl.ANY)
-    vmem = pl.BlockSpec(memory_space=pltpu.VMEM)
     dma = pltpu.SemaphoreType.DMA
     merged, grad_patch, grad_out = pl.pallas_call(
         kernel,
@@ -635,8 +653,14 @@
             jax.ShapeDtypeStruct((10, PIN), F32),
             jax.ShapeDtypeStruct((10, D), F32),
         ),
-        in_specs=[vmem] * 3,
-        out_specs=(vmem, vmem, vmem),
+        in_specs=[anywhere] * 3,
+        out_specs=(anywhere, anywhere, anywhere),
+        scratch_shapes=[
+            pltpu.VMEM((SEQ, D), BF),
+            pltpu.VMEM((10, PIN), F32),
+            pltpu.VMEM((10, D), F32),
+            dma((6,)),
+        ],
     )(merged, grad_patch, grad_out)
     return (merged, grad_patch.T, grad_out.T)
 

time: 62.1 us -> 61.2 us (0.986)
  Pallas kernels: 60.6 us -> 59.6 us
    pallas_call x1, Pallas kernels: 58.8 us -> 57.8 us  [shards(): pl.pallas_call(kernel, out_shape=(jax.ShapeDtypeStruct((SEQ, D), BF), jax...]
where the time goes in v8:
time: 61.2 us; the launch traced here: 61.1 us
  Pallas kernels  59.6 us (97%)
  between operations  1.45 us (2%)
    pallas_call x1, Pallas kernels, shards(): pl.pallas_call(kernel, out_shape=(jax.ShapeDtypeStruct((SEQ, D), BF), jax...  57.8 us
    pallas_call x1, Pallas kernels, shards(): pl.pallas_call(finish_kernel, out_shape=(jax.ShapeDtypeStruct((SEQ, D), B...  1.85 us

profile of v8, /device:TPU:1, one launch (start us, length us, event | category | flops | bytes accessed | tf_op | source)
XLA Modules:
  0.0 61.1 jit_solution(16319766853962111684)
XLA Ops:
  1.3 57.8 %shard_map.112 = (bf16[160,1280]{1,0:T(8,128)(2,1)}, f32[10,1152]{1,0:T(8,128)}, f32[10,1280]{1,0:T(8,128)}) custom-call(s32[1,128]{1,0:T(1,128)} %bitcast.3, s32[1,1]{1,0:T(1,128)S(6)} %copy.12.start_hbm, s32[128,1,128]{2,1,0:T(1,128)} %seg_hbm.1, bf16[128,1152]{1,0:T(8,128)(2,1)} %patches_hbm.1, bf16[160,1280]{1,0:T(8,128)(2,1)} %text_hbm.1, ...), custom_call_target="tpu_custom_call" | custom-call | tf_op jit(solution)/shard_map/pallas_call | solution.py:577
  59.0 1.8 %shard_map.113 = (bf16[160,1280]{1,0:T(8,128)(2,1)}, f32[10,1152]{1,0:T(8,128)}, f32[10,1280]{1,0:T(8,128)}) custom-call(bf16[160,1280]{1,0:T(8,128)(2,1)} %get-tuple-element.9.a, f32[10,1152]{1,0:T(8,128)} %get-tuple-element.10.b, f32[10,1280]{1,0:T(8,128)} %get-tuple-element.11.c), custom_call_target="tpu_custom_call" | custom-call | tf_op jit(solution)/shard_map/pallas_call | solution.py:649

commit v9 on v8

--- a/solution.py
+++ b/solution.py
@@ -487,6 +487,7 @@
         backward_heads(g)
 
 
+    exchange_second(1, emb_in, TN)
     mean_grad = jnp.zeros((1, ROWS), F32)
     mean_cross = jnp.zeros((1, ROWS), F32)
     for i in range(5):
@@ -496,7 +497,6 @@
         normed = (resT[rows, :] - mean) * inverse
         mean_grad = mean_grad + jnp.sum(tile, axis=0, keepdims=True)
         mean_cross = mean_cross + jnp.sum(tile * normed, axis=0, keepdims=True)
-    exchange_second(1, emb_in, TN)
     mean_grad = mean_grad * (1.0 / D)
     mean_cross = mean_cross * (1.0 / D)
 

time: 61.2 us -> 60.1 us (0.982)
  Pallas kernels: 59.6 us -> 58.6 us
    pallas_call x1, Pallas kernels: 57.8 us -> 56.7 us  [shards(): pl.pallas_call(kernel, out_shape=(jax.ShapeDtypeStruct((SEQ, D), BF), jax...]
where the time goes in v9:
time: 60.1 us; the launch traced here: 60 us
  Pallas kernels  58.6 us (98%)
  between operations  1.45 us (2%)
    pallas_call x1, Pallas kernels, shards(): pl.pallas_call(kernel, out_shape=(jax.ShapeDtypeStruct((SEQ, D), BF), jax...  56.7 us
    pallas_call x1, Pallas kernels, shards(): pl.pallas_call(finish_kernel, out_shape=(jax.ShapeDtypeStruct((SEQ, D), B...  1.85 us

profile of v9, /device:TPU:1, one launch (start us, length us, event | category | flops | bytes accessed | tf_op | source)
XLA Modules:
  0.0 60.0 jit_solution(7200301218874915102)
XLA Ops:
  1.3 56.7 %shard_map.112 = (bf16[160,1280]{1,0:T(8,128)(2,1)}, f32[10,1152]{1,0:T(8,128)}, f32[10,1280]{1,0:T(8,128)}) custom-call(s32[1,128]{1,0:T(1,128)} %bitcast.3, s32[1,1]{1,0:T(1,128)S(6)} %copy.12.start_hbm, s32[128,1,128]{2,1,0:T(1,128)} %seg_hbm.1, bf16[128,1152]{1,0:T(8,128)(2,1)} %patches_hbm.1, bf16[160,1280]{1,0:T(8,128)(2,1)} %text_hbm.1, ...), custom_call_target="tpu_custom_call" | custom-call | tf_op jit(solution)/shard_map/pallas_call | solution.py:577
  58.0 1.8 %shard_map.113 = (bf16[160,1280]{1,0:T(8,128)(2,1)}, f32[10,1152]{1,0:T(8,128)}, f32[10,1280]{1,0:T(8,128)}) custom-call(bf16[160,1280]{1,0:T(8,128)(2,1)} %get-tuple-element.9.a, f32[10,1152]{1,0:T(8,128)} %get-tuple-element.10.b, f32[10,1280]{1,0:T(8,128)} %get-tuple-element.11.c), custom_call_target="tpu_custom_call" | custom-call | tf_op jit(solution)/shard_map/pallas_call | solution.py:649
